TPU v7x, 512 devices: a whole 4x4x16 slice. The times are simulated.
512 devices in a mesh: blk: 32 (over y, z_lo, core), pw: 16 (over x, z_hi).
Axes of the slice: x: 4, y: 4, z: 16 (z_hi: 4, z_lo: 4; z = z_hi * 4 + z_lo), core: 2. Of those that a mesh axis runs over, the one named last changes fastest.
Arguments:
- res_pair: bfloat16 [65536, 12288], P('blk', 'pw'), may hold values from -0.56640625 to 0.56640625
- band_pair: bfloat16 [8192, 12288], P('blk', 'pw'), may hold values from -0.56640625 to 0.56640625
- coulomb: float32 [12288], P('pw'), may hold values from 0.2 to 5
- screening: float32 [2048], P('pw'), may hold values from 0.2 to 5
- val_form: bfloat16 [400, 2048], P(None, 'pw'), may hold values from -2.3125 to 2.3125
- cond_form: bfloat16 [600, 2048], P(None, 'pw'), may hold values from -2.3125 to 2.3125
- res_bands: int32 [3, 65536], P(None, 'blk'), may hold values from 0 to 299, as said below
- band_bands: int32 [3, 8192], P(None, 'blk'), may hold values from 0 to 299, as said below
Outputs:
- kernel: float32 [2, 65536, 256], P(None, ('blk', 'pw'))
Inputs may be any that keep to these rules, and one draw needn't show every extreme that they name: `res_bands`: row 0 holds valence bands below 200, row 1 conduction bands below 300, row 2 k-points below 2. `band_bands`: row 0 holds valence bands below 200, row 1 conduction bands below 300, row 2 k-points below 2.
All inputs are finite; a program needn't handle non-finite values.
Results may differ from a plain program's by a relative error of at most 0.01.
Values may be sent and summed in bfloat16 or wider, within the bound.
No kernel may reach another device: no remote copies, remote signals or barrier semaphores. Data moves between devices by JAX's collectives and lax.ppermute only.
A program may use at most 64 MiB of HBM per device.

v0:
```python
import jax
import jax.numpy as jnp
from jax import lax
from jax.sharding import PartitionSpec as P

NV = 200
NC = 300
STEPS = 2


def passed_along(x, axis, by):
    size = lax.axis_size(axis)
    return lax.ppermute(x, axis, [(i, (i + by) % size) for i in range(size)])


def make_density(bands, val_form, cond_form):
    rows_val = bands[2] * NV + bands[0]
    rows_cond = bands[2] * NC + bands[1]
    valence = jnp.take(val_form, rows_val, axis=0).astype(jnp.float32)
    conduct = jnp.take(cond_form, rows_cond, axis=0).astype(jnp.float32)
    return (valence * conduct).astype(jnp.bfloat16)


def contract_rows(left, right):
    return lax.dot_general(
        left, right, (((1,), (1,)), ((), ())), preferred_element_type=jnp.float32
    )


def make_term(res_pair, res_density, vis_weight, vis_screen):

    def term(start, count):
        return 2.0 * contract_rows(res_pair, vis_weight) - contract_rows(res_density, vis_screen)

    return term


def local(res_pair, band_pair, coulomb, screening, val_form, cond_form, res_bands, band_bands):
    res_density = make_density(res_bands, val_form, cond_form)
    band_density = make_density(band_bands, val_form, cond_form)
    weighted = (band_pair.astype(jnp.float32) * coulomb[None, :]).astype(jnp.bfloat16)
    screened = (band_density.astype(jnp.float32) * screening[None, :]).astype(jnp.bfloat16)
    own_rows = res_pair.shape[0] // lax.axis_size("pw")
    own_payload = (weighted, screened)
    payload = own_payload
    pieces = []
    for step_index in range(STEPS):
        payload = passed_along((payload[0], payload[1]), "blk", 1)
        vis_weight, vis_screen = payload
        term = make_term(res_pair, res_density, vis_weight, vis_screen)
        pieces.append(
            lax.psum_scatter(
                term(jnp.int32(0), own_rows * lax.axis_size("pw")),
                "pw",
                scatter_dimension=0,
                tiled=True,
            )
        )
    return jnp.stack(pieces, axis=0)


def solution(mesh):
    return jax.shard_map(
        local,
        mesh=mesh,
        in_specs=(
            P("blk", "pw"),
            P("blk", "pw"),
            P("pw"),
            P("pw"),
            P(None, "pw"),
            P(None, "pw"),
            P(None, "blk"),
            P(None, "blk"),
        ),
        out_specs=P(None, ("blk", "pw"), None),
        check_vma=False,
    )
```

profile of v0, /device:TPU:1, one launch (start us, length us, event | category | flops | bytes accessed | tf_op | source)
XLA Modules:
  0.0 306.3 jit_solution(6909597478380732383)
XLA Ops:
  6.5 0.0 copy-start
  6.5 0.0 reduce-scatter.3.cloned.1.call-start
  6.5 0.9 compare_select_fusion.5
  7.5 1.8 gather_fusion.2
  9.2 1.7 gather_fusion.3
  10.9 0.8 multiply_convert_fusion.2
  11.7 4.9 %collective-permute-start.1 = (bf16[256,128]{1,0:T(8,128)(2,1)S(1)}, bf16[256,128]{1,0:T(8,128)(2,1)S(1)}, u32[]{:S(2)}, u32[]{:S(2)}) collective-permute-start(bf16[256,128]{1,0:T(8,128)(2,1)S(1)} %multiply_convert_fusion.2), channel_id=1, source_target_pairs={{0,16},{16,32},{32,48},{48,64},{64,80},{80,96},{96,112},{112,128},... | collective-permute-start | bytes 196616 | tf_op jit(solution)/shard_map/ppermute | solution.py:13
  16.6 1.8 multiply_convert_fusion.1
  18.4 1.9 collective-permute-start
  20.4 0.0 copy-done.4
  20.4 0.6 compare_and_fusion
  21.0 0.0 copy-done.1
  21.0 8.0 %gather_fusion = bf16[2048,128]{1,0:T(8,128)(2,1)} fusion(bf16[400,128]{1,0:T(8,128)(2,1)S(1)} %copy-done.1, s32[2048]{0:T(1024)S(1)} %broadcast_clamp_fusion.1), kind=kCustom, calls=%fused_computation | custom fusion | bytes 1056768 | tf_op jit(solution)/shard_map/jit(_take)/gather | solution.py:19
  29.0 0.0 copy-done.2
  29.0 8.0 %gather_fusion.1 = bf16[2048,128]{1,0:T(8,128)(2,1)} fusion(bf16[600,128]{1,0:T(8,128)(2,1)S(1)} %copy-done.2, s32[2048]{0:T(1024)S(1)} %broadcast_clamp_fusion), kind=kCustom, calls=%fused_computation.1 | custom fusion | bytes 1056768 | tf_op jit(solution)/shard_map/jit(_take)/gather | solution.py:20
  37.0 0.0 collective-permute-done.1
  37.0 2.2 fusion.5
  39.2 0.0 collective-permute-done
  39.2 3.4 %fusion.3 = f32[2048,256]{0,1:T(8,128)} fusion(f32[2048,256]{0,1:T(8,128)S(1)} %fusion.5, bf16[256,768]{1,0:T(8,128)(2,1)} %collective-permute-done, bf16[2048,768]{1,0:T(8,128)(2,1)S(1)} %copy-done), kind=kOutput, calls=%fused_computation.9 | convolution fusion | flops 806354944 | bytes 7733248 | tf_op jit(solution)/shard_map/dot_general | solution.py:25
  42.6 0.0 reduce-scatter.3.cloned.1.call-update
  42.6 0.0 reduce-scatter.5.cloned.1.call-start
  42.7 3.9 %collective-permute-start.2 = (bf16[256,768]{1,0:T(8,128)(2,1)}, bf16[256,768]{1,0:T(8,128)(2,1)S(1)}, u32[]{:S(2)}, u32[]{:S(2)}) collective-permute-start(bf16[256,768]{1,0:T(8,128)(2,1)} %collective-permute-done), channel_id=1, source_target_pairs={{0,16},{16,32},{32,48},{48,64},{64,80},{80,96},{96,112},{112,128},... | collective-permute-start | bytes 1179656 | tf_op jit(solution)/shard_map/ppermute | solution.py:13
  46.6 1.9 collective-permute-start.3
  48.6 3.7 %collective-permute-done.3 = bf16[256,128]{1,0:T(8,128)(2,1)S(1)} collective-permute-done((bf16[256,128]{1,0:T(8,128)(2,1)S(1)}, bf16[256,128]{1,0:T(8,128)(2,1)S(1)}, u32[]{:S(2)}, u32[]{:S(2)}) %collective-permute-start.3) | collective-permute-done | bytes 65568 | tf_op jit(solution)/shard_map/ppermute | solution.py:13
  52.2 2.2 fusion.4
  54.4 0.0 collective-permute-done.2
  54.4 2.4 fusion.1
  56.8 0.0 reduce-scatter.5.cloned.1.call-update
  56.8 115.2 %reduce-scatter.3.cloned.1.call-done = f32[128,256]{0,1:T(8,128)} async-done(((f32[2048,256]{0,1:T(8,128)}), f32[128,256]{0,1:T(8,128)}) %reduce-scatter.3.cloned.1.call-update) | async-done | bytes 131088 | tf_op jit(solution)/shard_map/reduce_scatter | solution.py:52
  172.1 125.6 %reduce-scatter.5.cloned.1.call-done = f32[128,256]{0,1:T(8,128)} async-done(((f32[2048,256]{0,1:T(8,128)}), f32[128,256]{0,1:T(8,128)}) %reduce-scatter.5.cloned.1.call-update) | async-done | bytes 131088 | tf_op jit(solution)/shard_map/reduce_scatter | solution.py:52
  297.6 1.0 pad_maximum_fusion
  298.6 0.8 copy.14
  (12 shorter events, 0.1 us)
Async XLA Ops:
  6.5 32.7 %copy-start = (bf16[2048,768]{1,0:T(8,128)(2,1)S(1)}, bf16[2048,768]{1,0:T(8,128)(2,1)}, u32[]{:S(2)}) copy-start(bf16[2048,768]{1,0:T(8,128)(2,1)} %param.8) | copy-start | bytes 9437188
  6.5 14.5 %copy-start.1 = (bf16[400,128]{1,0:T(8,128)(2,1)S(1)}, bf16[400,128]{1,0:T(8,128)(2,1)}, u32[]{:S(2)}) copy-start(bf16[400,128]{1,0:T(8,128)(2,1)} %param.12) | copy-start | bytes 307204
  6.5 13.8 %copy-start.4 = (s32[3,2048]{1,0:T(4,128)S(1)}, s32[3,2048]{1,0:T(4,128)}, u32[]{:S(2)}) copy-start(s32[3,2048]{1,0:T(4,128)} %param.14) | copy-start | bytes 73732
  6.5 165.5 %reduce-scatter.3.cloned.1.call-start = ((), (), s32[]{:S(2)}) async-start(), calls=%async_computation.2 | async-start | bytes 2228224 | tf_op jit(solution)/shard_map/reduce_scatter | solution.py:52
  11.7 25.3 %collective-permute-start.1 = (bf16[256,128]{1,0:T(8,128)(2,1)S(1)}, bf16[256,128]{1,0:T(8,128)(2,1)S(1)}, u32[]{:S(2)}, u32[]{:S(2)}) collective-permute-start(bf16[256,128]{1,0:T(8,128)(2,1)S(1)} %multiply_convert_fusion.2), channel_id=1, source_target_pairs={{0,16},{16,32},{32,48},{48,64},{64,80},{80,96},{96,112},{112,128},... | collective-permute-start | bytes 196616 | tf_op jit(solution)/shard_map/ppermute | solution.py:13
  18.4 20.8 %collective-permute-start = (bf16[256,768]{1,0:T(8,128)(2,1)}, bf16[256,768]{1,0:T(8,128)(2,1)}, u32[]{:S(2)}, u32[]{:S(2)}) collective-permute-start(bf16[256,768]{1,0:T(8,128)(2,1)} %multiply_convert_fusion.1), channel_id=1, source_target_pairs={{0,16},{16,32},{32,48},{48,64},{64,80},{80,96},{96,112},{112,128},... | collective-permute-start | bytes 1179656 | tf_op jit(solution)/shard_map/ppermute | solution.py:13
  21.0 8.0 %copy-start.2 = (bf16[600,128]{1,0:T(8,128)(2,1)S(1)}, bf16[600,128]{1,0:T(8,128)(2,1)}, u32[]{:S(2)}) copy-start(bf16[600,128]{1,0:T(8,128)(2,1)} %param.13) | copy-start | bytes 460804
  29.0 8.0 %copy-start.3 = (pred[2048]{0:T(1024)(128)(4,1)S(1)}, pred[2048]{0:T(1024)(128)(4,1)}, u32[]{:S(2)}) copy-start(pred[2048]{0:T(1024)(128)(4,1)} %get-tuple-element.20) | copy-start | bytes 6148
  42.6 255.0 %reduce-scatter.5.cloned.1.call-start = ((), (), s32[]{:S(2)}) async-start(), calls=%async_computation.3 | async-start | bytes 2228224 | tf_op jit(solution)/shard_map/reduce_scatter | solution.py:52
  42.7 11.8 %collective-permute-start.2 = (bf16[256,768]{1,0:T(8,128)(2,1)}, bf16[256,768]{1,0:T(8,128)(2,1)S(1)}, u32[]{:S(2)}, u32[]{:S(2)}) collective-permute-start(bf16[256,768]{1,0:T(8,128)(2,1)} %collective-permute-done), channel_id=1, source_target_pairs={{0,16},{16,32},{32,48},{48,64},{64,80},{80,96},{96,112},{112,128},... | collective-permute-start | bytes 1179656 | tf_op jit(solution)/shard_map/ppermute | solution.py:13
  46.6 5.6 %collective-permute-start.3 = (bf16[256,128]{1,0:T(8,128)(2,1)S(1)}, bf16[256,128]{1,0:T(8,128)(2,1)S(1)}, u32[]{:S(2)}, u32[]{:S(2)}) collective-permute-start(bf16[256,128]{1,0:T(8,128)(2,1)S(1)} %collective-permute-done.1), channel_id=1, source_target_pairs={{0,16},{16,32},{32,48},{48,64},{64,80},{80,96},{96,112},{112,128},... | collective-permute-start | bytes 196616 | tf_op jit(solution)/shard_map/ppermute | solution.py:13
Sparse Core Ops, SparseCore 0:
  42.7 129.2 reduce-scatter.2
  176.8 120.8 reduce-scatter.4
where the time goes:
time: 307 us; the launch traced here: 306 us
  waiting for transfers between devices  245 us (80%)
  local copies, waits for them, and re-layouts  20.2 us (7%)
  between operations  13.5 us (4%)
  starting transfers between devices  12.7 us (4%)
  matrix products  10.1 us (3%)
  other arithmetic  5.13 us (2%)
    reduce_scatter x2, waiting for transfers between devices, local(): lax.psum_scatter(term(jnp.int32(0), own_rows * lax.axis_size('pw')), 'pw'...  241 us
    ppermute x4, starting transfers between devices, passed_along(): return lax.ppermute(x, axis, [(i, (i + by) % size) for i in range(size)])  12.7 us
    dot_general x4, matrix products, contract_rows(): lax.dot_general(left, right, (((1,), (1,)), ((), ())), preferred_element_...  10.1 us
    gather x2, local copies, waits for them, and re-layouts, make_density(): valence = jnp.take(val_form, rows_val, axis=0).astype(jnp.float32)  9.74 us
    gather x2, local copies, waits for them, and re-layouts, make_density(): conduct = jnp.take(cond_form, rows_cond, axis=0).astype(jnp.float32)  9.65 us
  transfers between devices with their start and end apart: 6, of which 3 were waited for; matrix products, arithmetic and copies ran while one was open for 8% of the time, Pallas kernels for 0%

commit v1 on v0

v1 whole, which is shorter than its diff:
```python
import functools

import jax
import jax.numpy as jnp
from jax import lax
from jax.experimental import pallas as pl
from jax.experimental.pallas import tpu as pltpu
from jax.sharding import PartitionSpec as P

NV = 200
NC = 300
N_X = 4
N_Z = 4
X_GROUPS = [[x * N_Z + z for x in range(N_X)] for z in range(N_Z)]
F32 = jnp.float32
BF16 = jnp.bfloat16
VMEM_LIMIT = 63 * 2**20
ANY = pl.BlockSpec(memory_space=pl.ANY)
SMEM = pl.BlockSpec(memory_space=pltpu.SMEM)
INDEX_ROWS = 16
OUTWARD = (2, 3)
INWARD = (1, 0)


def swapped_along_z(x, by):
    pairs = [(a * N_Z + z, a * N_Z + (z ^ by)) for a in range(N_X) for z in range(N_Z)]
    return lax.ppermute(x, "pw", pairs)


def call(kernel, name, out_shape, in_specs, scratch, flops):
    return pl.pallas_call(
        kernel,
        in_specs=in_specs,
        out_specs=jax.tree.map(lambda _: ANY, out_shape),
        out_shape=out_shape,
        scratch_shapes=scratch,
        compiler_params=pltpu.CompilerParams(vmem_limit_bytes=VMEM_LIMIT),
        cost_estimate=pl.CostEstimate(flops=flops, bytes_accessed=10**6, transcendentals=0),
        name=name,
    )


def picked_rows(form, rows):
    hits = lax.broadcasted_iota(jnp.int32, (rows.shape[0], form.shape[0]), 1) == rows
    return jnp.dot(hits.astype(F32).astype(BF16), form, preferred_element_type=F32)


def density(rows_val, rows_cond, val_form, cond_form):
    rows = jnp.concatenate([rows_val, rows_cond] * 4, axis=0).T
    picked = picked_rows(val_form, rows[:, 0:1]) * picked_rows(cond_form, rows[:, 1:2])
    return picked.astype(BF16)


def res_kernel(
    z_ref, pair_ref, val_ref, cond_ref, bands_ref, out_ref, in_ref, bands, val, cond, pair, dens, sems
):
    rows, groups = pair.shape
    own = rows // (N_X * N_Z)
    tables = table_copies((bands_ref, val_ref, cond_ref), (bands, val, cond), sems, 0)
    for copy in tables:
        copy.start()
    read = pltpu.make_async_copy(pair_ref, pair, sems.at[3])
    read.start()
    for copy in tables:
        copy.wait()
    rows_val = bands[2:3, :] * NV + bands[0:1, :]
    rows_cond = bands[2:3, :] * NC + bands[1:2, :]
    dens[...] = density(rows_val, rows_cond, val[...], cond[...])
    read.wait()
    gives = []
    for ref, steps in ((out_ref, OUTWARD), (in_ref, INWARD)):
        for x in range(N_X):
            for k, m in enumerate(steps):
                source = pl.ds(pl.multiple_of((x * N_Z + (z_ref[0] ^ m)) * own, own), own)
                target = ref.at[pl.ds((x * len(steps) + k) * own, own), :]
                at = 4 + 2 * len(gives) // 2
                gives.append(
                    pltpu.make_async_copy(
                        pair.at[source, :], target.at[:, pl.ds(0, groups)], sems.at[at]
                    )
                )
                gives.append(
                    pltpu.make_async_copy(
                        dens.at[source, :],
                        target.at[:, pl.ds(groups, dens.shape[1])],
                        sems.at[at + 1],
                    )
                )
    for give in gives:
        give.start()
    for give in gives:
        give.wait()


def table_copies(refs, places, sems, first):
    return [
        pltpu.make_async_copy(ref, place, sems.at[first + k])
        for k, (ref, place) in enumerate(zip(refs, places, strict=True))
    ]


def band_payload(band_pair, band_bands):
    rows_val = band_bands[2] * NV + band_bands[0]
    rows_cond = band_bands[2] * NC + band_bands[1]
    parts = jnp.stack([rows_val // 4, rows_val % 4, rows_cond // 4, rows_cond % 4])
    groups = band_pair.shape[1]
    parts = jnp.pad(parts, ((0, INDEX_ROWS - 4), (0, groups - parts.shape[1])))
    return jnp.concatenate([band_pair, parts.astype(BF16)], axis=0)


def product(left, right):
    return lax.dot_general(
        left, right, (((1,), (1,)), ((), ())), preferred_element_type=F32
    ).astype(BF16)


def out_kernel(
    odd_ref, left_ref, far_ref, even_ref, from_odd_ref, coulomb_ref, screening_ref, val_ref,
    cond_ref, out_ref, band_ref, near, far, coulomb, screening, val, cond, left, band, out, sems,
):
    cols, groups = near.shape[0] - INDEX_ROWS, near.shape[1]

    @pl.when(odd_ref[0] == 0)
    def _():
        pltpu.make_async_copy(from_odd_ref, near, sems.at[0]).start()

    @pl.when(odd_ref[0] != 0)
    def _():
        pltpu.make_async_copy(even_ref, near, sems.at[0]).start()

    refs = (far_ref, coulomb_ref, screening_ref, val_ref, cond_ref)
    copies = table_copies(refs, (far, coulomb, screening, val, cond), sems, 1)
    for copy in copies:
        copy.start()
    rows = pltpu.make_async_copy(left_ref, left, sems.at[6])
    rows.start()
    pltpu.make_async_copy(from_odd_ref, near, sems.at[0]).wait()
    for copy in copies:
        copy.wait()
    parts = jnp.concatenate([near[cols:, :cols], far[cols:, :cols]], axis=1)
    parts = parts.astype(F32).astype(jnp.int32)
    rows_val = parts[0:1, :] * 4 + parts[1:2, :]
    rows_cond = parts[2:3, :] * 4 + parts[3:4, :]
    dens = density(rows_val, rows_cond, val[...], cond[...])
    band[:, groups:] = -((dens.astype(F32) * screening[...]).astype(BF16))
    for k, payload in enumerate((near, far)):
        weighted = (payload[:cols, :].astype(F32) * coulomb[...]).astype(BF16)
        band[k * cols : (k + 1) * cols, :groups] = weighted * 2
    keep = pltpu.make_async_copy(band, band_ref, sems.at[0])
    keep.start()
    rows.wait()
    give_product(left, band, out, out_ref, sems)
    keep.wait()


def give_product(left, band, out, out_ref, sems, blocks=2):
    gives = []
    size = out.shape[0] // blocks
    for k in range(blocks):
        at = pl.ds(k * size, size)
        out[at, :] = product(left[at, :], band[...])
        gives.append(pltpu.make_async_copy(out.at[at, :], out_ref.at[at, :], sems.at[1 + k]))
        gives[-1].start()
    for give in gives:
        give.wait()


def in_kernel(left_ref, band_ref, out_ref, left, band, out, sems):
    rows = table_copies((left_ref, band_ref), (left, band), sems, 0)
    for copy in rows:
        copy.start()
    for copy in rows:
        copy.wait()
    give_product(left, band, out, out_ref, sems)


def shares_over_x(part):
    rows, cols = part.shape
    return lax.all_to_all(
        part.reshape(N_X, rows // N_X, cols), "pw", 0, 0, axis_index_groups=X_GROUPS
    )


def local(res_pair, band_pair, coulomb, screening, val_form, cond_form, res_bands, band_bands):
    rows, groups = res_pair.shape
    cols = band_pair.shape[0]
    depth = groups + val_form.shape[1]
    own = rows // (N_X * N_Z)
    half = rows // 2
    blocks = lax.axis_size("blk")
    payload = band_payload(band_pair, band_bands)
    far = lax.ppermute(payload, "blk", [(i, (i + 2) % blocks) for i in range(blocks)])
    from_even = lax.ppermute(payload, "blk", [(i, i + 1) for i in range(0, blocks, 2)])

    z = (lax.axis_index("pw") % N_Z).astype(jnp.int32)[None]
    odd = (lax.axis_index("blk") % 2).astype(jnp.int32)[None]
    tables = (coulomb[None, :], screening[None, :], val_form, cond_form)
    form_scratch = [pltpu.VMEM(t.shape, t.dtype) for t in tables]
    left = pltpu.VMEM((half, depth), BF16)
    band = pltpu.VMEM((2 * cols, depth), BF16)
    out = pltpu.VMEM((half, 2 * cols), BF16)
    block = pltpu.VMEM(payload.shape, BF16)
    left_shape = jax.ShapeDtypeStruct((half, depth), BF16)
    band_shape = jax.ShapeDtypeStruct((2 * cols, depth), BF16)
    term_shape = jax.ShapeDtypeStruct((half, 2 * cols), BF16)
    left_out, left_in = call(
        res_kernel,
        "res_rows",
        (left_shape, left_shape),
        [SMEM] + [ANY] * 4,
        [
            pltpu.VMEM(res_bands.shape, jnp.int32),
            *form_scratch[2:],
            pltpu.VMEM((rows, groups), BF16),
            pltpu.VMEM((rows, depth - groups), BF16),
            pltpu.SemaphoreType.DMA((4 + 4 * N_X * N_Z,)),
        ],
        2 * 10**9,
    )(z, res_pair, val_form, cond_form, res_bands)
    far, left_out, left_in, odd, tables = lax.optimization_barrier(
        (far, left_out, left_in, odd, tables)
    )
    from_odd = lax.ppermute(far, "blk", [(i + 1, i) for i in range(0, blocks, 2)])
    out_term, bands = call(
        out_kernel,
        "out_term",
        (term_shape, band_shape),
        [SMEM] + [ANY] * 8,
        [block, block, *form_scratch, left, band, out, pltpu.SemaphoreType.DMA((8,))],
        2 * 10**9,
    )(odd, left_out, far, from_even, from_odd, *tables)
    in_term = call(
        in_kernel,
        "in_term",
        term_shape,
        [ANY] * 2,
        [left, band, out, pltpu.SemaphoreType.DMA((4,))],
        2 * 10**9,
    )(left_in, bands)

    shares = shares_over_x(out_term)
    to_2 = jnp.sum(shares[:, :own].astype(F32), axis=0).astype(BF16)
    to_3 = jnp.sum(shares[:, own:].astype(F32), axis=0).astype(BF16)
    in_term, shares = lax.optimization_barrier((in_term, shares))
    from_2 = swapped_along_z(to_2, 2)
    from_3 = swapped_along_z(to_3, 3)
    shares = shares_over_x(in_term)
    to_1 = jnp.sum(shares[:, :own].astype(F32), axis=0).astype(BF16)
    from_1 = swapped_along_z(to_1, 1)
    total = jnp.sum(shares[:, own:].astype(F32), axis=0)
    total = total + from_2.astype(F32) + from_3.astype(F32) + from_1.astype(F32)
    return total.reshape(own, 2, cols).transpose(1, 0, 2)


def solution(mesh):
    return jax.shard_map(
        local,
        mesh=mesh,
        in_specs=(
            P("blk", "pw"),
            P("blk", "pw"),
            P("pw"),
            P("pw"),
            P(None, "pw"),
            P(None, "pw"),
            P(None, "blk"),
            P(None, "blk"),
        ),
        out_specs=P(None, ("blk", "pw"), None),
        check_vma=False,
    )
```

time: 307 us -> 89.6 us (0.29)
  waiting for transfers between devices: 245 us -> 26.7 us
  starting transfers between devices: 12.7 us -> 42.4 us
  local copies, waits for them, and re-layouts: 20.2 us -> 2.24 us
  Pallas kernels: 0 us -> 13.8 us
  between operations: 13.5 us -> 0.17 us
  matrix products: 10.1 us -> 0 us
    reduce_scatter x2 -> x0, waiting for transfers between devices: 241 us -> none  [local(): lax.psum_scatter(term(jnp.int32(0), own_rows * lax.axis_size('pw')), 'pw'...]
    ppermute x4 -> x6, starting transfers between devices: 12.7 us -> 34.6 us  [the longest x3 20.5 us: swapped_along_z(): return lax.ppermute(x, 'pw', pairs)]
    gather x4 -> x0, local copies, waits for them, and re-layouts: 19.4 us -> none  [the longest x2 9.74 us: make_density(): valence = jnp.take(val_form, rows_val, axis=0).astype(jnp.float32)]
    pallas_call x0 -> x3, Pallas kernels: none -> 13.8 us  [the longest x1 5.45 us: local(): call(res_kernel, 'res_rows', (left_shape, left_shape), [SMEM] + [ANY] * 4...]
    ppermute x4 -> x6, waiting for transfers between devices: 3.69 us -> 15.7 us  [the longest x3 12.5 us: swapped_along_z(): return lax.ppermute(x, 'pw', pairs)]
    all_to_all x0 -> x2, waiting for transfers between devices: none -> 11 us  [shares_over_x(): lax.all_to_all(part.reshape(N_X, rows // N_X, cols), 'pw', 0, 0, axis_ind...]
    dot_general x4 -> x0, matrix products: 10.1 us -> none  [contract_rows(): lax.dot_general(left, right, (((1,), (1,)), ((), ())), preferred_element_...]
    all_to_all x0 -> x2, starting transfers between devices: none -> 7.79 us  [shares_over_x(): lax.all_to_all(part.reshape(N_X, rows // N_X, cols), 'pw', 0, 0, axis_ind...]
  transfers between devices with their start and end apart: 6 -> 8, of which waited for: 3 -> 5; matrix products, arithmetic and copies ran while one was open for 8% -> 3% of each run, Pallas kernels for 0% -> 11%
where the time goes in v1:
time: 89.6 us; the launch traced here: 88.9 us
  starting transfers between devices  42.4 us (47%)
  waiting for transfers between devices  26.7 us (30%)
  Pallas kernels  13.8 us (15%)
  other arithmetic  3.53 us (4%)
  local copies, waits for them, and re-layouts  2.24 us (3%)
    ppermute x3, starting transfers between devices, swapped_along_z(): return lax.ppermute(x, 'pw', pairs)  20.5 us
    ppermute x3, waiting for transfers between devices, swapped_along_z(): return lax.ppermute(x, 'pw', pairs)  12.5 us
    all_to_all x2, waiting for transfers between devices, shares_over_x(): lax.all_to_all(part.reshape(N_X, rows // N_X, cols), 'pw', 0, 0, axis_ind...  11 us
    ppermute x1, starting transfers between devices, local(): lax.ppermute(far, 'blk', [(i + 1, i) for i in range(0, blocks, 2)])  8.44 us
    all_to_all x2, starting transfers between devices, shares_over_x(): lax.all_to_all(part.reshape(N_X, rows // N_X, cols), 'pw', 0, 0, axis_ind...  7.79 us
    pallas_call x1, Pallas kernels, local(): call(res_kernel, 'res_rows', (left_shape, left_shape), [SMEM] + [ANY] * 4...  5.45 us
    pallas_call x1, Pallas kernels, local(): call(out_kernel, 'out_term', (term_shape, band_shape), [SMEM] + [ANY] * 8...  4.5 us
    ppermute x1, starting transfers between devices, local(): lax.ppermute(payload, 'blk', [(i, (i + 2) % blocks) for i in range(blocks)])  4.38 us
  transfers between devices with their start and end apart: 8, of which 5 were waited for; matrix products, arithmetic and copies ran while one was open for 3% of the time, Pallas kernels for 11%

profile of v1, /device:TPU:1, one launch (start us, length us, event | category | flops | bytes accessed | tf_op | source)
XLA Modules:
  0.0 88.9 jit_solution(10883878950228294123)
XLA Ops:
  0.0 0.8 slice_add_fusion.1
  0.9 1.0 %pad_maximum_fusion = bf16[272,768]{1,0:T(8,128)(2,1)S(1)} fusion(bf16[16,768]{1,0:T(8,128)(2,1)S(1)} %fusion.8, bf16[256,768]{1,0:T(8,128)(2,1)} %param.9), kind=kLoop, calls=%fused_computation.4 | loop fusion | flops 835584 | bytes 835584 | tf_op jit(solution)/shard_map/concatenate | solution.py:108
  1.9 4.4 %collective-permute-start = (bf16[272,768]{1,0:T(8,128)(2,1)S(1)}, bf16[272,768]{1,0:T(8,128)(2,1)S(1)}, u32[]{:S(2)}, u32[]{:S(2)}) collective-permute-start(bf16[272,768]{1,0:T(8,128)(2,1)S(1)} %pad_maximum_fusion), channel_id=1, source_target_pairs={{0,32},{16,48},{32,64},{48,80},{64,96},{80,112},{96,128},{112,144}... | collective-permute-start | bytes 1253384 | tf_op jit(solution)/shard_map/ppermute | solution.py:192
  6.3 1.3 %collective-permute-start.1 = (bf16[272,768]{1,0:T(8,128)(2,1)S(1)}, bf16[272,768]{1,0:T(8,128)(2,1)}, u32[]{:S(2)}, u32[]{:S(2)}) collective-permute-start(bf16[272,768]{1,0:T(8,128)(2,1)S(1)} %pad_maximum_fusion), channel_id=1, source_target_pairs={{0,16},{32,48},{64,80},{96,112},{128,144},{160,176},{192,208},{224... | collective-permute-start | bytes 1253384 | tf_op jit(solution)/shard_map/ppermute | solution.py:193
  7.6 1.3 %broadcast_in_dim.14.coulomb_ref = f32[1,768]{1,0:T(1,128)} reshape(f32[768]{0:T(1024)} %param.10) | data formatting | bytes 6144 | tf_op jit(solution)/shard_map/broadcast_in_dim | solution.py:197
  8.9 5.5 %res_rows.1 = (bf16[1024,896]{1,0:T(8,128)(2,1)}, bf16[1024,896]{1,0:T(8,128)(2,1)}) custom-call(s32[1]{0:T(128)} %bitcast.z_ref, bf16[2048,768]{1,0:T(8,128)(2,1)} %pair_ref.1, bf16[400,128]{1,0:T(8,128)(2,1)} %val_ref.2, bf16[600,128]{1,0:T(8,128)(2,1)} %cond_ref.2, s32[3,2048]{1,0:T(4,128)} %bands_ref.1), custom_call_target="tpu_custom_call" | custom-call | flops 2000000000 | bytes 1000000 | tf_op jit(solution)/shard_map/res_rows/pallas_call | solution.py:206
  14.3 2.5 %collective-permute-done.far_ref = bf16[272,768]{1,0:T(8,128)(2,1)S(1)} collective-permute-done((bf16[272,768]{1,0:T(8,128)(2,1)S(1)}, bf16[272,768]{1,0:T(8,128)(2,1)S(1)}, u32[]{:S(2)}, u32[]{:S(2)}) %collective-permute-start) | collective-permute-done | bytes 417824 | tf_op jit(solution)/shard_map/ppermute | solution.py:192
  16.9 0.0 copy-start
  16.9 8.4 %collective-permute-start.2 = (bf16[272,768]{1,0:T(8,128)(2,1)S(1)}, bf16[272,768]{1,0:T(8,128)(2,1)}, u32[]{:S(2)}, u32[]{:S(2)}) collective-permute-start(bf16[272,768]{1,0:T(8,128)(2,1)S(1)} %collective-permute-done.far_ref), channel_id=1, source_target_pairs={{16,0},{48,32},{80,64},{112,96},{144,128},{176,160},{208,192},{240... | collective-permute-start | bytes 1253384 | tf_op jit(solution)/shard_map/ppermute | solution.py:223
  25.3 0.0 collective-permute-done.1.even_ref
  25.3 0.7 collective-permute-done.2.from_odd_ref
  26.0 0.0 copy-done
  26.0 4.5 %out_term.1 = (bf16[1024,512]{1,0:T(8,128)(2,1)}, bf16[512,896]{1,0:T(8,128)(2,1)}) custom-call(s32[1]{0:T(128)} %bitcast.1.odd_ref, bf16[1024,896]{1,0:T(8,128)(2,1)} %get-tuple-element.22.left_ref, bf16[272,768]{1,0:T(8,128)(2,1)} %copy-done, bf16[272,768]{1,0:T(8,128)(2,1)} %collective-permute-done.1.even_ref, ...), custom_call_target="tpu_custom_call" | custom-call | flops 2000000000 | bytes 1000000 | tf_op jit(solution)/shard_map/out_term/pallas_call | solution.py:224
  30.5 4.3 %all-to-all-start = ((bf16[4,256,512]{2,1,0:T(8,128)(2,1)}), bf16[4,256,512]{2,1,0:T(8,128)(2,1)}, u32[]{:S(2)}, u32[]{:S(2)}) async-start(bf16[4,256,512]{2,1,0:T(8,128)(2,1)} %bitcast.9), calls=%async_computation | async-start | bytes 2097152 | tf_op jit(solution)/shard_map/all_to_all | solution.py:179
  34.8 3.9 %in_term.1 = bf16[1024,512]{1,0:T(8,128)(2,1)} custom-call(bf16[1024,896]{1,0:T(8,128)(2,1)} %get-tuple-element.20.left_ref, bf16[512,896]{1,0:T(8,128)(2,1)} %get-tuple-element.28.band_ref), custom_call_target="tpu_custom_call" | custom-call | flops 2000000000 | bytes 1000000 | tf_op jit(solution)/shard_map/in_term/pallas_call | solution.py:232
  38.7 11.0 %all-to-all-done = bf16[4,256,512]{2,1,0:T(8,128)(2,1)} async-done(((bf16[4,256,512]{2,1,0:T(8,128)(2,1)}), bf16[4,256,512]{2,1,0:T(8,128)(2,1)}, u32[]{:S(2)}, u32[]{:S(2)}) %all-to-all-start) | async-done | bytes 1048608 | tf_op jit(solution)/shard_map/all_to_all | solution.py:179
  49.7 3.5 %all-to-all-start.1 = ((bf16[4,256,512]{2,1,0:T(8,128)(2,1)}), bf16[4,256,512]{2,1,0:T(8,128)(2,1)S(1)}, u32[]{:S(2)}, u32[]{:S(2)}) async-start(bf16[4,256,512]{2,1,0:T(8,128)(2,1)} %bitcast.8), calls=%async_computation.1 | async-start | bytes 2097152 | tf_op jit(solution)/shard_map/all_to_all | solution.py:179
  53.3 1.4 %slice_reduce_fusion.2 = (bf16[128,512]{1,0:T(8,128)(2,1)S(1)}, bf16[128,512]{1,0:T(8,128)(2,1)S(1)}) fusion(bf16[4,256,512]{2,1,0:T(8,128)(2,1)} %all-to-all-done), kind=kLoop, calls=%fused_computation.3 | loop fusion | flops 393216 | bytes 1310720 | tf_op jit(solution)/shard_map/reduce_sum | solution.py:242
  54.7 13.3 %collective-permute-start.3 = (bf16[128,512]{1,0:T(8,128)(2,1)S(1)}, bf16[128,512]{1,0:T(8,128)(2,1)S(1)}, u32[]{:S(2)}, u32[]{:S(2)}) collective-permute-start(bf16[128,512]{1,0:T(8,128)(2,1)S(1)} %get-tuple-element.31), channel_id=1, source_target_pairs={{0,2},{1,3},{2,0},{3,1},{4,6},{5,7},{6,4},{7,5},{8,10},{9,11},{10,... | collective-permute-start | bytes 393224 | tf_op jit(solution)/shard_map/ppermute | solution.py:27
  68.0 1.9 %collective-permute-start.4 = (bf16[128,512]{1,0:T(8,128)(2,1)S(1)}, bf16[128,512]{1,0:T(8,128)(2,1)S(1)}, u32[]{:S(2)}, u32[]{:S(2)}) collective-permute-start(bf16[128,512]{1,0:T(8,128)(2,1)S(1)} %get-tuple-element.32), channel_id=1, source_target_pairs={{0,3},{1,2},{2,1},{3,0},{4,7},{5,6},{6,5},{7,4},{8,11},{9,10},{10,... | collective-permute-start | bytes 393224 | tf_op jit(solution)/shard_map/ppermute | solution.py:27
  70.0 0.0 all-to-all-done.1
  70.0 0.1 slice_reduce_fusion
  70.1 5.2 %collective-permute-start.5 = (bf16[128,512]{1,0:T(8,128)(2,1)S(1)}, bf16[128,512]{1,0:T(8,128)(2,1)S(1)}, u32[]{:S(2)}, u32[]{:S(2)}) collective-permute-start(bf16[128,512]{1,0:T(8,128)(2,1)S(1)} %slice_reduce_fusion), channel_id=1, source_target_pairs={{0,1},{1,0},{2,3},{3,2},{4,5},{5,4},{6,7},{7,6},{8,9},{9,8},{10,11... | collective-permute-start | bytes 393224 | tf_op jit(solution)/shard_map/ppermute | solution.py:27
  75.3 0.1 convert_reduce_fusion
  75.4 0.0 collective-permute-done.3
  75.4 11.4 %collective-permute-done.4 = bf16[128,512]{1,0:T(8,128)(2,1)S(1)} collective-permute-done((bf16[128,512]{1,0:T(8,128)(2,1)S(1)}, bf16[128,512]{1,0:T(8,128)(2,1)S(1)}, u32[]{:S(2)}, u32[]{:S(2)}) %collective-permute-start.4) | collective-permute-done | bytes 131104 | tf_op jit(solution)/shard_map/ppermute | solution.py:27
  86.7 1.1 %collective-permute-done.5 = bf16[128,512]{1,0:T(8,128)(2,1)S(1)} collective-permute-done((bf16[128,512]{1,0:T(8,128)(2,1)S(1)}, bf16[128,512]{1,0:T(8,128)(2,1)S(1)}, u32[]{:S(2)}, u32[]{:S(2)}) %collective-permute-start.5) | collective-permute-done | bytes 131104 | tf_op jit(solution)/shard_map/ppermute | solution.py:27
  87.9 0.1 convert_add_fusion
  87.9 0.1 copy.10
  88.1 0.8 copy.11
  (4 shorter events, 0.0 us)
Async XLA Ops:
  1.9 15.0 %collective-permute-start = (bf16[272,768]{1,0:T(8,128)(2,1)S(1)}, bf16[272,768]{1,0:T(8,128)(2,1)S(1)}, u32[]{:S(2)}, u32[]{:S(2)}) collective-permute-start(bf16[272,768]{1,0:T(8,128)(2,1)S(1)} %pad_maximum_fusion), channel_id=1, source_target_pairs={{0,32},{16,48},{32,64},{48,80},{64,96},{80,112},{96,128},{112,144}... | collective-permute-start | bytes 1253384 | tf_op jit(solution)/shard_map/ppermute | solution.py:192
  6.3 19.0 %collective-permute-start.1 = (bf16[272,768]{1,0:T(8,128)(2,1)S(1)}, bf16[272,768]{1,0:T(8,128)(2,1)}, u32[]{:S(2)}, u32[]{:S(2)}) collective-permute-start(bf16[272,768]{1,0:T(8,128)(2,1)S(1)} %pad_maximum_fusion), channel_id=1, source_target_pairs={{0,16},{32,48},{64,80},{96,112},{128,144},{160,176},{192,208},{224... | collective-permute-start | bytes 1253384 | tf_op jit(solution)/shard_map/ppermute | solution.py:193
  16.9 9.2 %copy-start = (bf16[272,768]{1,0:T(8,128)(2,1)}, bf16[272,768]{1,0:T(8,128)(2,1)S(1)}, u32[]{:S(2)}) copy-start(bf16[272,768]{1,0:T(8,128)(2,1)S(1)} %collective-permute-done.far_ref) | copy-start | bytes 1253380
  16.9 9.2 %collective-permute-start.2 = (bf16[272,768]{1,0:T(8,128)(2,1)S(1)}, bf16[272,768]{1,0:T(8,128)(2,1)}, u32[]{:S(2)}, u32[]{:S(2)}) collective-permute-start(bf16[272,768]{1,0:T(8,128)(2,1)S(1)} %collective-permute-done.far_ref), channel_id=1, source_target_pairs={{16,0},{48,32},{80,64},{112,96},{144,128},{176,160},{208,192},{240... | collective-permute-start | bytes 1253384 | tf_op jit(solution)/shard_map/ppermute | solution.py:223
  30.5 19.2 %all-to-all-start = ((bf16[4,256,512]{2,1,0:T(8,128)(2,1)}), bf16[4,256,512]{2,1,0:T(8,128)(2,1)}, u32[]{:S(2)}, u32[]{:S(2)}) async-start(bf16[4,256,512]{2,1,0:T(8,128)(2,1)} %bitcast.9), calls=%async_computation | async-start | bytes 2097152 | tf_op jit(solution)/shard_map/all_to_all | solution.py:179
  49.7 20.2 %all-to-all-start.1 = ((bf16[4,256,512]{2,1,0:T(8,128)(2,1)}), bf16[4,256,512]{2,1,0:T(8,128)(2,1)S(1)}, u32[]{:S(2)}, u32[]{:S(2)}) async-start(bf16[4,256,512]{2,1,0:T(8,128)(2,1)} %bitcast.8), calls=%async_computation.1 | async-start | bytes 2097152 | tf_op jit(solution)/shard_map/all_to_all | solution.py:179
  54.7 20.7 %collective-permute-start.3 = (bf16[128,512]{1,0:T(8,128)(2,1)S(1)}, bf16[128,512]{1,0:T(8,128)(2,1)S(1)}, u32[]{:S(2)}, u32[]{:S(2)}) collective-permute-start(bf16[128,512]{1,0:T(8,128)(2,1)S(1)} %get-tuple-element.31), channel_id=1, source_target_pairs={{0,2},{1,3},{2,0},{3,1},{4,6},{5,7},{6,4},{7,5},{8,10},{9,11},{10,... | collective-permute-start | bytes 393224 | tf_op jit(solution)/shard_map/ppermute | solution.py:27
  68.0 18.7 %collective-permute-start.4 = (bf16[128,512]{1,0:T(8,128)(2,1)S(1)}, bf16[128,512]{1,0:T(8,128)(2,1)S(1)}, u32[]{:S(2)}, u32[]{:S(2)}) collective-permute-start(bf16[128,512]{1,0:T(8,128)(2,1)S(1)} %get-tuple-element.32), channel_id=1, source_target_pairs={{0,3},{1,2},{2,1},{3,0},{4,7},{5,6},{6,5},{7,4},{8,11},{9,10},{10,... | collective-permute-start | bytes 393224 | tf_op jit(solution)/shard_map/ppermute | solution.py:27
  70.1 17.8 %collective-permute-start.5 = (bf16[128,512]{1,0:T(8,128)(2,1)S(1)}, bf16[128,512]{1,0:T(8,128)(2,1)S(1)}, u32[]{:S(2)}, u32[]{:S(2)}) collective-permute-start(bf16[128,512]{1,0:T(8,128)(2,1)S(1)} %slice_reduce_fusion), channel_id=1, source_target_pairs={{0,1},{1,0},{2,3},{3,2},{4,5},{5,4},{6,7},{7,6},{8,9},{9,8},{10,11... | collective-permute-start | bytes 393224 | tf_op jit(solution)/shard_map/ppermute | solution.py:27

commit v2 on v1

v2 whole, which is shorter than its diff:
```python
import functools

import jax
import jax.numpy as jnp
from jax import lax
from jax.experimental import pallas as pl
from jax.experimental.pallas import tpu as pltpu
from jax.sharding import PartitionSpec as P

NV = 200
NC = 300
N_X = 4
N_Z = 4
X_GROUPS = [[x * N_Z + z for x in range(N_X)] for z in range(N_Z)]
F32 = jnp.float32
BF16 = jnp.bfloat16
VMEM_LIMIT = 63 * 2**20
ANY = pl.BlockSpec(memory_space=pl.ANY)
INDEX_ROWS = 16
FIRST_ROWS = (2, 0)
OTHER_ROWS = (1, 3)


def along_z(x, by):
    pairs = [(a * N_Z + z, a * N_Z + (z + by) % N_Z) for a in range(N_X) for z in range(N_Z)]
    return lax.ppermute(x, "pw", pairs)


def call(kernel, name, out_shape, in_specs, scratch, flops):
    return pl.pallas_call(
        kernel,
        in_specs=in_specs,
        out_specs=jax.tree.map(lambda _: ANY, out_shape),
        out_shape=out_shape,
        scratch_shapes=scratch,
        compiler_params=pltpu.CompilerParams(vmem_limit_bytes=VMEM_LIMIT),
        cost_estimate=pl.CostEstimate(flops=flops, bytes_accessed=10**6, transcendentals=0),
        name=name,
    )


def picked_rows(form, rows):
    hits = lax.broadcasted_iota(jnp.int32, (rows.shape[0], form.shape[0]), 1) == rows
    return jnp.dot(hits.astype(F32).astype(BF16), form, preferred_element_type=F32)


def density(rows_val, rows_cond, val_form, cond_form):
    rows = jnp.concatenate([rows_val, rows_cond] * 4, axis=0).T
    picked = picked_rows(val_form, rows[:, 0:1]) * picked_rows(cond_form, rows[:, 1:2])
    return picked.astype(BF16)


def res_kernel(
    pair_ref, val_ref, cond_ref, bands_ref, out_ref, in_ref, bands, val, cond, pair, dens, sems
):
    rows, groups = pair.shape
    own = rows // (N_X * N_Z)
    pw = lax.axis_index("pw")
    my_x, my_z = pw // N_Z, pw % N_Z
    tables = table_copies((bands_ref, val_ref, cond_ref), (bands, val, cond), sems, 0)
    for copy in tables:
        copy.start()
    reads = split_copies(pair_ref, pair, sems, 4, 4)
    for read in reads:
        read.start()
    for copy in tables:
        copy.wait()
    rows_val = bands[2:3, :] * NV + bands[0:1, :]
    rows_cond = bands[2:3, :] * NC + bands[1:2, :]
    dens[...] = density(rows_val, rows_cond, val[...], cond[...])
    for read in reads:
        read.wait()
    gives = []
    for ref, steps in ((out_ref, FIRST_ROWS), (in_ref, OTHER_ROWS)):
        for x in range(N_X):
            for k, m in enumerate(steps):
                owner_x = x if ref is out_ref else (x + my_x) % N_X
                owner = owner_x * N_Z + (my_z + m) % N_Z
                source = pl.ds(pl.multiple_of(owner * own, own), own)
                target = ref.at[pl.ds((x * len(steps) + k) * own, own), :]
                at = 4 + 2 * len(gives) // 2
                gives.append(
                    pltpu.make_async_copy(
                        pair.at[source, :], target.at[:, pl.ds(0, groups)], sems.at[at]
                    )
                )
                gives.append(
                    pltpu.make_async_copy(
                        dens.at[source, :],
                        target.at[:, pl.ds(groups, dens.shape[1])],
                        sems.at[at + 1],
                    )
                )
    for give in gives:
        give.start()
    for give in gives:
        give.wait()


def split_copies(source, target, sems, first, count):
    size = source.shape[0] // count
    return [
        pltpu.make_async_copy(
            source.at[pl.ds(k * size, size), :], target.at[pl.ds(k * size, size), :], sems.at[first + k]
        )
        for k in range(count)
    ]


def table_copies(refs, places, sems, first):
    return [
        pltpu.make_async_copy(ref, place, sems.at[first + k])
        for k, (ref, place) in enumerate(zip(refs, places, strict=True))
    ]


def payload_kernel(pair_ref, bands_ref, out_ref, bands, sems):
    cols, groups = pair_ref.shape
    read = pltpu.make_async_copy(bands_ref, bands, sems.at[0])
    read.start()
    moves = split_copies(pair_ref, out_ref.at[pl.ds(0, cols), :], sems, 1, 4)
    for move in moves:
        move.start()
    read.wait()
    rows_val = bands[2:3, :] * NV + bands[0:1, :]
    rows_cond = bands[2:3, :] * NC + bands[1:2, :]
    codes = [rows_val // 4, rows_val % 4, rows_cond // 4, rows_cond % 4]
    codes = jnp.concatenate(codes * (INDEX_ROWS // 4), axis=0)
    codes = jnp.concatenate([codes] * (groups // cols), axis=1)
    out_ref[cols:, :] = codes.astype(F32).astype(BF16)
    for move in moves:
        move.wait()


def band_payload(band_pair, band_bands):
    cols, groups = band_pair.shape
    return pl.pallas_call(
        payload_kernel,
        in_specs=[ANY] * 2,
        out_specs=pl.BlockSpec(memory_space=pltpu.VMEM),
        out_shape=jax.ShapeDtypeStruct((cols + INDEX_ROWS, groups), BF16),
        scratch_shapes=[
            pltpu.VMEM(band_bands.shape, jnp.int32),
            pltpu.SemaphoreType.DMA((5,)),
        ],
        compiler_params=pltpu.CompilerParams(vmem_limit_bytes=60 * 2**20),
        cost_estimate=pl.CostEstimate(flops=10**7, bytes_accessed=10**6, transcendentals=0),
        name="band_payload",
    )(band_pair, band_bands)


def product(left, right):
    return lax.dot_general(
        left, right, (((1,), (1,)), ((), ())), preferred_element_type=F32
    ).astype(BF16)


def out_kernel(
    left_ref, far_ref, even_ref, from_odd_ref, coulomb_ref, screening_ref, val_ref,
    cond_ref, out_ref, band_ref, near, far, coulomb, screening, val, cond, left, band, out, sems,
):
    cols, groups = near.shape[0] - INDEX_ROWS, near.shape[1]

    odd = lax.axis_index("blk") % 2

    @pl.when(odd == 0)
    def _():
        pltpu.make_async_copy(from_odd_ref, near, sems.at[0]).start()

    @pl.when(odd != 0)
    def _():
        pltpu.make_async_copy(even_ref, near, sems.at[0]).start()

    refs = (far_ref, coulomb_ref, screening_ref, val_ref, cond_ref)
    copies = table_copies(refs, (far, coulomb, screening, val, cond), sems, 1)
    for copy in copies:
        copy.start()
    rows = split_copies(left_ref, left, sems, 6, 4)
    for row in rows:
        row.start()
    pltpu.make_async_copy(from_odd_ref, near, sems.at[0]).wait()
    for copy in copies:
        copy.wait()
    parts = jnp.concatenate([near[cols:, :cols], far[cols:, :cols]], axis=1)
    parts = parts.astype(F32).astype(jnp.int32)
    rows_val = parts[0:1, :] * 4 + parts[1:2, :]
    rows_cond = parts[2:3, :] * 4 + parts[3:4, :]
    dens = density(rows_val, rows_cond, val[...], cond[...])
    band[:, groups:] = -((dens.astype(F32) * screening[...][None, :]).astype(BF16))
    for k, payload in enumerate((near, far)):
        weighted = (payload[:cols, :].astype(F32) * coulomb[...][None, :]).astype(BF16)
        band[k * cols : (k + 1) * cols, :groups] = weighted * 2
    keep = pltpu.make_async_copy(band, band_ref, sems.at[0])
    keep.start()
    for row in rows:
        row.wait()
    half = out.shape[0] // 2
    halves = (out_ref.at[pl.ds(0, half)], out_ref.at[pl.ds(half, half)])
    give_product(left, band, out, halves, sems)
    keep.wait()


def give_product(left, band, out, out_refs, sems):
    gives = []
    count, steps, own, cols = out.shape
    each = count // len(out_refs)
    for k, ref in enumerate(out_refs):
        total = product(left[pl.ds(k * each * own, each * own), :], band[...])
        for n in range(each):
            for step in range(steps):
                out[k * each + n, step] = total[
                    n * own : (n + 1) * own, step * cols : (step + 1) * cols
                ]
        gives.append(pltpu.make_async_copy(out.at[pl.ds(k * each, each)], ref, sems.at[1 + k]))
        gives[-1].start()
    for give in gives:
        give.wait()


def in_kernel(left_ref, band_ref, out_0, out_1, out_2, out_3, left, band, out, sems):
    rows = split_copies(left_ref, left, sems, 5, 4) + split_copies(band_ref, band, sems, 9, 2)
    for copy in rows:
        copy.start()
    for copy in rows:
        copy.wait()
    give_product(left, band, out, (out_0, out_1, out_2, out_3), sems)


def along_x(x, by):
    pairs = [(a * N_Z + z, (a + by) % N_X * N_Z + z) for a in range(N_X) for z in range(N_Z)]
    return lax.ppermute(x, "pw", pairs)


def shares_over_x(pieces):
    return lax.all_to_all(pieces, "pw", 0, 0, axis_index_groups=X_GROUPS, tiled=True)


def local(res_pair, band_pair, coulomb, screening, val_form, cond_form, res_bands, band_bands):
    rows, groups = res_pair.shape
    cols = band_pair.shape[0]
    depth = groups + val_form.shape[1]
    own = rows // (N_X * N_Z)
    few, many = (rows * len(steps) // N_Z for steps in (FIRST_ROWS, OTHER_ROWS))
    blocks = lax.axis_size("blk")
    payload = band_payload(band_pair, band_bands)
    far = lax.ppermute(payload, "blk", [(i, (i + 2) % blocks) for i in range(blocks)])
    from_even = lax.ppermute(payload, "blk", [(i, i + 1) for i in range(0, blocks, 2)])

    tables = (coulomb, screening, val_form, cond_form)
    form_scratch = [pltpu.VMEM(t.shape, t.dtype) for t in tables]
    band = pltpu.VMEM((2 * cols, depth), BF16)
    block = pltpu.VMEM(payload.shape, BF16)
    band_shape = jax.ShapeDtypeStruct((2 * cols, depth), BF16)
    left_out, left_in = call(
        res_kernel,
        "res_rows",
        tuple(jax.ShapeDtypeStruct((n, depth), BF16) for n in (few, many)),
        [ANY] * 4,
        [
            pltpu.VMEM(res_bands.shape, jnp.int32),
            *form_scratch[2:],
            pltpu.VMEM((rows, groups), BF16),
            pltpu.VMEM((rows, depth - groups), BF16),
            pltpu.SemaphoreType.DMA((4 + 4 * N_X * N_Z,)),
        ],
        2 * 10**9,
    )(res_pair, val_form, cond_form, res_bands)
    far, left_out, left_in, tables = lax.optimization_barrier((far, left_out, left_in, tables))
    from_odd = lax.ppermute(far, "blk", [(i + 1, i) for i in range(0, blocks, 2)])
    out_term, bands = call(
        out_kernel,
        "out_term",
        (jax.ShapeDtypeStruct((few // own, 2, own, cols), BF16), band_shape),
        [ANY] * 8,
        [
            block,
            block,
            *form_scratch,
            pltpu.VMEM((few, depth), BF16),
            band,
            pltpu.VMEM((few // own, 2, own, cols), BF16),
            pltpu.SemaphoreType.DMA((10,)),
        ],
        2 * 10**9,
    )(left_out, far, from_even, from_odd, *tables)
    in_terms = call(
        in_kernel,
        "in_term",
        (jax.ShapeDtypeStruct((len(OTHER_ROWS), 2, own, cols), BF16),) * N_X,
        [ANY] * 2,
        [
            pltpu.VMEM((many, depth), BF16),
            band,
            pltpu.VMEM((many // own, 2, own, cols), BF16),
            pltpu.SemaphoreType.DMA((11,)),
        ],
        2 * 10**9,
    )(left_in, bands)

    first_shares = shares_over_x(out_term)
    to_2 = jnp.sum(first_shares[0::2].astype(F32), axis=0).astype(BF16)
    from_2 = along_z(to_2, 2)
    own_share, _ = lax.optimization_barrier((in_terms[0], to_2))
    shares = [own_share] + [along_x(in_terms[by], by) for by in (1, 3, 2)]

    def summed(k):
        return sum(s[k].astype(F32) for s in shares)

    to_1, to_3 = summed(0).astype(BF16), summed(1).astype(BF16)
    from_1 = along_z(to_1, 1)
    from_3 = along_z(to_3, 3)
    first_shares, _, _ = lax.optimization_barrier((first_shares, to_1, to_3))
    total = jnp.sum(first_shares[1::2].astype(F32), axis=0)
    total, from_2 = lax.optimization_barrier((total, from_2))
    return total + from_2.astype(F32) + from_1.astype(F32) + from_3.astype(F32)


def solution(mesh):
    return jax.shard_map(
        local,
        mesh=mesh,
        in_specs=(
            P("blk", "pw"),
            P("blk", "pw"),
            P("pw"),
            P("pw"),
            P(None, "pw"),
            P(None, "pw"),
            P(None, "blk"),
            P(None, "blk"),
        ),
        out_specs=P(None, ("blk", "pw"), None),
        check_vma=False,
    )
```

time: 89.6 us -> 88.1 us (0.983)
  waiting for transfers between devices: 26.7 us -> 16.6 us
  starting transfers between devices: 42.4 us -> 51 us
  local copies, waits for them, and re-layouts: 2.24 us -> 0.05 us
  Pallas kernels: 13.8 us -> 15.6 us
    ppermute x3 -> x6, starting transfers between devices: 20.5 us -> 32.6 us  [the longest x3 22.5 us: along_z(): return lax.ppermute(x, 'pw', pairs)]
    all_to_all x2 -> x1, waiting for transfers between devices: 11 us -> 1.05 us  [shares_over_x(): lax.all_to_all(pieces, 'pw', 0, 0, axis_index_groups=X_GROUPS, tiled=True)]
    all_to_all x2 -> x1, starting transfers between devices: 7.79 us -> 4.27 us  [shares_over_x(): lax.all_to_all(pieces, 'pw', 0, 0, axis_index_groups=X_GROUPS, tiled=True)]
    pallas_call x3 -> x4, Pallas kernels: 13.8 us -> 15.6 us  [the longest x1 5.45 us: local(): call(res_kernel, 'res_rows', tuple((jax.ShapeDtypeStruct((n, depth), BF16...]
    ppermute x3 -> x6, waiting for transfers between devices: 12.5 us -> 10.8 us  [the longest x3 10.8 us: along_z(): return lax.ppermute(x, 'pw', pairs)]
    ppermute x1, waiting for transfers between devices: 2.53 us -> 4.02 us  [local(): lax.ppermute(payload, 'blk', [(i, (i + 2) % blocks) for i in range(blocks)])]
    broadcast_in_dim x1 -> x0, local copies, waits for them, and re-layouts: 1.27 us -> none  [local(): tables = (coulomb[None, :], screening[None, :], val_form, cond_form)]
    concatenate x1 -> x0, other arithmetic: 1.03 us -> none  [band_payload(): return jnp.concatenate([band_pair, parts.astype(BF16)], axis=0)]
  transfers between devices with their start and end apart: 8 -> 10, of which waited for: 5 -> 5; matrix products, arithmetic and copies ran while one was open for 3% -> 4% of each run, Pallas kernels for 11% -> 11%
where the time goes in v2:
time: 88.1 us; the launch traced here: 87.5 us
  starting transfers between devices  51 us (58%)
  waiting for transfers between devices  16.6 us (19%)
  Pallas kernels  15.6 us (18%)
  other arithmetic  4.12 us (5%)
    ppermute x3, starting transfers between devices, along_z(): return lax.ppermute(x, 'pw', pairs)  22.5 us
    ppermute x3, waiting for transfers between devices, along_z(): return lax.ppermute(x, 'pw', pairs)  10.8 us
    ppermute x3, starting transfers between devices, along_x(): return lax.ppermute(x, 'pw', pairs)  10.1 us
    ppermute x1, starting transfers between devices, local(): lax.ppermute(far, 'blk', [(i + 1, i) for i in range(0, blocks, 2)])  8.43 us
    pallas_call x1, Pallas kernels, local(): call(res_kernel, 'res_rows', tuple((jax.ShapeDtypeStruct((n, depth), BF16...  5.45 us
    pallas_call x1, Pallas kernels, local(): call(out_kernel, 'out_term', (jax.ShapeDtypeStruct((few // own, 2, own, c...  4.53 us
    ppermute x1, starting transfers between devices, local(): lax.ppermute(payload, 'blk', [(i, (i + 2) % blocks) for i in range(blocks)])  4.37 us
    all_to_all x1, starting transfers between devices, shares_over_x(): lax.all_to_all(pieces, 'pw', 0, 0, axis_index_groups=X_GROUPS, tiled=True)  4.27 us
  transfers between devices with their start and end apart: 10, of which 5 were waited for; matrix products, arithmetic and copies ran while one was open for 4% of the time, Pallas kernels for 11%

profile of v2, /device:TPU:1, one launch (start us, length us, event | category | flops | bytes accessed | tf_op | source)
XLA Modules:
  0.0 87.5 jit_solution(8729873964042303580)
XLA Ops:
  0.0 1.9 %band_payload.1 = bf16[272,768]{1,0:T(8,128)(2,1)} custom-call(bf16[256,768]{1,0:T(8,128)(2,1)} %pair_ref.2, s32[3,256]{1,0:T(4,128)} %bands_ref.2), custom_call_target="tpu_custom_call" | custom-call | flops 10000000 | bytes 1000000 | tf_op jit(solution)/shard_map/band_payload/pallas_call | solution.py:137
  1.9 4.4 %collective-permute-start = (bf16[272,768]{1,0:T(8,128)(2,1)}, bf16[272,768]{1,0:T(8,128)(2,1)S(1)}, u32[]{:S(2)}, u32[]{:S(2)}) collective-permute-start(bf16[272,768]{1,0:T(8,128)(2,1)} %band_payload.1), channel_id=1, source_target_pairs={{0,32},{16,48},{32,64},{48,80},{64,96},{80,112},{96,128},{112,144}... | collective-permute-start | bytes 1253384 | tf_op jit(solution)/shard_map/ppermute | solution.py:246
  6.2 1.3 %collective-permute-start.1 = (bf16[272,768]{1,0:T(8,128)(2,1)}, bf16[272,768]{1,0:T(8,128)(2,1)S(1)}, u32[]{:S(2)}, u32[]{:S(2)}) collective-permute-start(bf16[272,768]{1,0:T(8,128)(2,1)} %band_payload.1), channel_id=1, source_target_pairs={{0,16},{32,48},{64,80},{96,112},{128,144},{160,176},{192,208},{224... | collective-permute-start | bytes 1253384 | tf_op jit(solution)/shard_map/ppermute | solution.py:247
  7.5 5.5 %res_rows.1 = (bf16[1024,896]{1,0:T(8,128)(2,1)}, bf16[1024,896]{1,0:T(8,128)(2,1)}) custom-call(bf16[2048,768]{1,0:T(8,128)(2,1)} %pair_ref.3, bf16[400,128]{1,0:T(8,128)(2,1)} %val_ref.2, bf16[600,128]{1,0:T(8,128)(2,1)} %cond_ref.2, s32[3,2048]{1,0:T(4,128)} %bands_ref.3), custom_call_target="tpu_custom_call" | custom-call | flops 2000000000 | bytes 1000000 | tf_op jit(solution)/shard_map/res_rows/pallas_call | solution.py:254
  13.0 4.0 %collective-permute-done.far_ref = bf16[272,768]{1,0:T(8,128)(2,1)S(1)} collective-permute-done((bf16[272,768]{1,0:T(8,128)(2,1)}, bf16[272,768]{1,0:T(8,128)(2,1)S(1)}, u32[]{:S(2)}, u32[]{:S(2)}) %collective-permute-start) | collective-permute-done | bytes 417824 | tf_op jit(solution)/shard_map/ppermute | solution.py:246
  17.0 0.0 copy-start
  17.0 8.4 %collective-permute-start.2 = (bf16[272,768]{1,0:T(8,128)(2,1)S(1)}, bf16[272,768]{1,0:T(8,128)(2,1)}, u32[]{:S(2)}, u32[]{:S(2)}) collective-permute-start(bf16[272,768]{1,0:T(8,128)(2,1)S(1)} %collective-permute-done.far_ref), channel_id=1, source_target_pairs={{16,0},{48,32},{80,64},{112,96},{144,128},{176,160},{208,192},{240... | collective-permute-start | bytes 1253384 | tf_op jit(solution)/shard_map/ppermute | solution.py:269
  25.5 0.0 collective-permute-done.1.even_ref
  25.5 0.0 copy-start.1
  25.5 0.7 collective-permute-done.2.from_odd_ref
  26.2 0.0 copy-done
  26.2 0.0 copy-done.1
  26.2 4.5 %out_term.1 = (bf16[8,2,128,256]{3,2,1,0:T(8,128)(2,1)}, bf16[512,896]{1,0:T(8,128)(2,1)}) custom-call(bf16[1024,896]{1,0:T(8,128)(2,1)} %get-tuple-element.26.left_ref, bf16[272,768]{1,0:T(8,128)(2,1)} %copy-done, bf16[272,768]{1,0:T(8,128)(2,1)} %copy-done.1, bf16[272,768]{1,0:T(8,128)(2,1)} %collective-permute-done.2.from_odd_ref, f32[768]{0:T(1024)} %coulomb_ref, ...), custom_call_target="tpu_custom_call" | custom-call | flops 2000000000 | bytes 1000000 | tf_op jit(solution)/shard_map/out_term/pallas_call | solution.py:270
  30.8 4.3 %all-to-all-start = ((bf16[8,2,128,256]{3,2,1,0:T(8,128)(2,1)}), bf16[8,2,128,256]{3,2,1,0:T(8,128)(2,1)}, u32[]{:S(2)}, u32[]{:S(2)}) async-start(bf16[8,2,128,256]{3,2,1,0:T(8,128)(2,1)} %get-tuple-element.32), calls=%async_computation | async-start | bytes 2097152 | tf_op jit(solution)/shard_map/all_to_all | solution.py:235
  35.1 3.8 %in_term.1 = (bf16[2,2,128,256]{3,2,1,0:T(8,128)(2,1)}, bf16[2,2,128,256]{3,2,1,0:T(8,128)(2,1)}, bf16[2,2,128,256]{3,2,1,0:T(8,128)(2,1)}, bf16[2,2,128,256]{3,2,1,0:T(8,128)(2,1)}) custom-call(bf16[1024,896]{1,0:T(8,128)(2,1)} %get-tuple-element.33.left_ref, bf16[512,896]{1,0:T(8,128)(2,1)} %get-tuple-element.34.band_ref), custom_call_target="tpu_custom_call" | custom-call | flops 2000000000 | bytes 1000000 | tf_op jit(solution)/shard_map/in_term/pallas_call | solution.py:286
  38.9 3.3 %collective-permute-start.3 = (bf16[2,2,128,256]{3,2,1,0:T(8,128)(2,1)}, bf16[2,2,128,256]{3,2,1,0:T(8,128)(2,1)S(1)}, u32[]{:S(2)}, u32[]{:S(2)}) collective-permute-start(bf16[2,2,128,256]{3,2,1,0:T(8,128)(2,1)} %get-tuple-element.37), channel_id=1, source_target_pairs={{0,4},{1,5},{2,6},{3,7},{4,8},{5,9},{6,10},{7,11},{8,12},{9,13},{1... | collective-permute-start | bytes 786440 | tf_op jit(solution)/shard_map/ppermute | solution.py:231
  42.2 3.2 %collective-permute-start.4 = (bf16[2,2,128,256]{3,2,1,0:T(8,128)(2,1)}, bf16[2,2,128,256]{3,2,1,0:T(8,128)(2,1)S(1)}, u32[]{:S(2)}, u32[]{:S(2)}) collective-permute-start(bf16[2,2,128,256]{3,2,1,0:T(8,128)(2,1)} %get-tuple-element.38), channel_id=1, source_target_pairs={{0,12},{1,13},{2,14},{3,15},{4,0},{5,1},{6,2},{7,3},{8,4},{9,5},{1... | collective-permute-start | bytes 786440 | tf_op jit(solution)/shard_map/ppermute | solution.py:231
  45.4 3.6 %collective-permute-start.5 = (bf16[2,2,128,256]{3,2,1,0:T(8,128)(2,1)}, bf16[2,2,128,256]{3,2,1,0:T(8,128)(2,1)S(1)}, u32[]{:S(2)}, u32[]{:S(2)}) collective-permute-start(bf16[2,2,128,256]{3,2,1,0:T(8,128)(2,1)} %get-tuple-element.39), channel_id=1, source_target_pairs={{0,8},{1,9},{2,10},{3,11},{4,12},{5,13},{6,14},{7,15},{8,0},{9,1},... | collective-permute-start | bytes 786440 | tf_op jit(solution)/shard_map/ppermute | solution.py:231
  49.0 1.1 %all-to-all-done = bf16[8,2,128,256]{3,2,1,0:T(8,128)(2,1)} async-done(((bf16[8,2,128,256]{3,2,1,0:T(8,128)(2,1)}), bf16[8,2,128,256]{3,2,1,0:T(8,128)(2,1)}, u32[]{:S(2)}, u32[]{:S(2)}) %all-to-all-start) | async-done | bytes 1048608 | tf_op jit(solution)/shard_map/all_to_all | solution.py:235
  50.1 1.1 %slice_reduce_fusion = bf16[2,128,256]{2,1,0:T(8,128)(2,1)S(1)} fusion(bf16[8,2,128,256]{3,2,1,0:T(8,128)(2,1)} %all-to-all-done), kind=kLoop, calls=%fused_computation.1 | loop fusion | flops 196608 | bytes 655360 | tf_op jit(solution)/shard_map/reduce_sum | solution.py:301
  51.2 13.3 %collective-permute-start.6 = (bf16[2,128,256]{2,1,0:T(8,128)(2,1)S(1)}, bf16[2,128,256]{2,1,0:T(8,128)(2,1)S(1)}, u32[]{:S(2)}, u32[]{:S(2)}) collective-permute-start(bf16[2,128,256]{2,1,0:T(8,128)(2,1)S(1)} %slice_reduce_fusion), channel_id=1, source_target_pairs={{0,2},{1,3},{2,0},{3,1},{4,6},{5,7},{6,4},{7,5},{8,10},{9,11},{10,... | collective-permute-start | bytes 393224 | tf_op jit(solution)/shard_map/ppermute | solution.py:26
  64.5 0.0 collective-permute-done.3
  64.5 0.0 collective-permute-done.4
  64.5 0.0 collective-permute-done.5
  64.5 1.1 %fusion = (bf16[2,128,256]{2,1,0:T(8,128)(2,1)S(1)}, bf16[2,128,256]{2,1,0:T(8,128)(2,1)S(1)}) fusion(bf16[2,2,128,256]{3,2,1,0:T(8,128)(2,1)S(1)} %collective-permute-done.5, bf16[2,2,128,256]{3,2,1,0:T(8,128)(2,1)S(1)} %collective-permute-done.4, bf16[2,2,128,256]{3,2,1,0:T(8,128)(2,1)S(1)} %collective-permute-done.3, ...), kind=kLoop, calls=%fused_computation.5 | loop fusion | flops 1048576 | bytes 1310720 | tf_op jit(solution)/shard_map/add | solution.py:307
  65.6 4.8 %collective-permute-start.7 = (bf16[2,128,256]{2,1,0:T(8,128)(2,1)S(1)}, bf16[2,128,256]{2,1,0:T(8,128)(2,1)S(1)}, u32[]{:S(2)}, u32[]{:S(2)}) collective-permute-start(bf16[2,128,256]{2,1,0:T(8,128)(2,1)S(1)} %get-tuple-element.43), channel_id=1, source_target_pairs={{0,1},{1,2},{2,3},{3,0},{4,5},{5,6},{6,7},{7,4},{8,9},{9,10},{10,1... | collective-permute-start | bytes 393224 | tf_op jit(solution)/shard_map/ppermute | solution.py:26
  70.4 4.4 %collective-permute-start.8 = (bf16[2,128,256]{2,1,0:T(8,128)(2,1)S(1)}, bf16[2,128,256]{2,1,0:T(8,128)(2,1)S(1)}, u32[]{:S(2)}, u32[]{:S(2)}) collective-permute-start(bf16[2,128,256]{2,1,0:T(8,128)(2,1)S(1)} %get-tuple-element.44), channel_id=1, source_target_pairs={{0,3},{1,0},{2,1},{3,2},{4,7},{5,4},{6,5},{7,6},{8,11},{9,8},{10,9... | collective-permute-start | bytes 393224 | tf_op jit(solution)/shard_map/ppermute | solution.py:26
  74.9 1.1 %convert_reduce_fusion = f32[2,128,256]{2,1,0:T(8,128)S(1)} fusion(bf16[8,2,128,256]{3,2,1,0:T(8,128)(2,1)} %all-to-all-done), kind=kLoop, calls=%fused_computation | loop fusion | flops 458752 | bytes 786432 | tf_op jit(solution)/shard_map/reduce_sum | solution.py:313
  76.0 0.0 collective-permute-done.6
  76.0 5.4 %collective-permute-done.7 = bf16[2,128,256]{2,1,0:T(8,128)(2,1)S(1)} collective-permute-done((bf16[2,128,256]{2,1,0:T(8,128)(2,1)S(1)}, bf16[2,128,256]{2,1,0:T(8,128)(2,1)S(1)}, u32[]{:S(2)}, u32[]{:S(2)}) %collective-permute-start.7) | collective-permute-done | bytes 131104 | tf_op jit(solution)/shard_map/ppermute | solution.py:26
  81.5 5.3 %collective-permute-done.8 = bf16[2,128,256]{2,1,0:T(8,128)(2,1)S(1)} collective-permute-done((bf16[2,128,256]{2,1,0:T(8,128)(2,1)S(1)}, bf16[2,128,256]{2,1,0:T(8,128)(2,1)S(1)}, u32[]{:S(2)}, u32[]{:S(2)}) %collective-permute-start.8) | collective-permute-done | bytes 131104 | tf_op jit(solution)/shard_map/ppermute | solution.py:26
  86.8 0.8 convert_add_fusion
Async XLA Ops:
  1.9 15.2 %collective-permute-start = (bf16[272,768]{1,0:T(8,128)(2,1)}, bf16[272,768]{1,0:T(8,128)(2,1)S(1)}, u32[]{:S(2)}, u32[]{:S(2)}) collective-permute-start(bf16[272,768]{1,0:T(8,128)(2,1)} %band_payload.1), channel_id=1, source_target_pairs={{0,32},{16,48},{32,64},{48,80},{64,96},{80,112},{96,128},{112,144}... | collective-permute-start | bytes 1253384 | tf_op jit(solution)/shard_map/ppermute | solution.py:246
  6.2 19.2 %collective-permute-start.1 = (bf16[272,768]{1,0:T(8,128)(2,1)}, bf16[272,768]{1,0:T(8,128)(2,1)S(1)}, u32[]{:S(2)}, u32[]{:S(2)}) collective-permute-start(bf16[272,768]{1,0:T(8,128)(2,1)} %band_payload.1), channel_id=1, source_target_pairs={{0,16},{32,48},{64,80},{96,112},{128,144},{160,176},{192,208},{224... | collective-permute-start | bytes 1253384 | tf_op jit(solution)/shard_map/ppermute | solution.py:247
  17.0 9.2 %copy-start = (bf16[272,768]{1,0:T(8,128)(2,1)}, bf16[272,768]{1,0:T(8,128)(2,1)S(1)}, u32[]{:S(2)}) copy-start(bf16[272,768]{1,0:T(8,128)(2,1)S(1)} %collective-permute-done.far_ref) | copy-start | bytes 1253380
  17.0 9.2 %collective-permute-start.2 = (bf16[272,768]{1,0:T(8,128)(2,1)S(1)}, bf16[272,768]{1,0:T(8,128)(2,1)}, u32[]{:S(2)}, u32[]{:S(2)}) collective-permute-start(bf16[272,768]{1,0:T(8,128)(2,1)S(1)} %collective-permute-done.far_ref), channel_id=1, source_target_pairs={{16,0},{48,32},{80,64},{112,96},{144,128},{176,160},{208,192},{240... | collective-permute-start | bytes 1253384 | tf_op jit(solution)/shard_map/ppermute | solution.py:269
  25.5 0.8 copy-start.1
  30.8 19.3 %all-to-all-start = ((bf16[8,2,128,256]{3,2,1,0:T(8,128)(2,1)}), bf16[8,2,128,256]{3,2,1,0:T(8,128)(2,1)}, u32[]{:S(2)}, u32[]{:S(2)}) async-start(bf16[8,2,128,256]{3,2,1,0:T(8,128)(2,1)} %get-tuple-element.32), calls=%async_computation | async-start | bytes 2097152 | tf_op jit(solution)/shard_map/all_to_all | solution.py:235
  38.9 25.6 %collective-permute-start.3 = (bf16[2,2,128,256]{3,2,1,0:T(8,128)(2,1)}, bf16[2,2,128,256]{3,2,1,0:T(8,128)(2,1)S(1)}, u32[]{:S(2)}, u32[]{:S(2)}) collective-permute-start(bf16[2,2,128,256]{3,2,1,0:T(8,128)(2,1)} %get-tuple-element.37), channel_id=1, source_target_pairs={{0,4},{1,5},{2,6},{3,7},{4,8},{5,9},{6,10},{7,11},{8,12},{9,13},{1... | collective-permute-start | bytes 786440 | tf_op jit(solution)/shard_map/ppermute | solution.py:231
  42.2 22.3 %collective-permute-start.4 = (bf16[2,2,128,256]{3,2,1,0:T(8,128)(2,1)}, bf16[2,2,128,256]{3,2,1,0:T(8,128)(2,1)S(1)}, u32[]{:S(2)}, u32[]{:S(2)}) collective-permute-start(bf16[2,2,128,256]{3,2,1,0:T(8,128)(2,1)} %get-tuple-element.38), channel_id=1, source_target_pairs={{0,12},{1,13},{2,14},{3,15},{4,0},{5,1},{6,2},{7,3},{8,4},{9,5},{1... | collective-permute-start | bytes 786440 | tf_op jit(solution)/shard_map/ppermute | solution.py:231
  45.4 19.2 %collective-permute-start.5 = (bf16[2,2,128,256]{3,2,1,0:T(8,128)(2,1)}, bf16[2,2,128,256]{3,2,1,0:T(8,128)(2,1)S(1)}, u32[]{:S(2)}, u32[]{:S(2)}) collective-permute-start(bf16[2,2,128,256]{3,2,1,0:T(8,128)(2,1)} %get-tuple-element.39), channel_id=1, source_target_pairs={{0,8},{1,9},{2,10},{3,11},{4,12},{5,13},{6,14},{7,15},{8,0},{9,1},... | collective-permute-start | bytes 786440 | tf_op jit(solution)/shard_map/ppermute | solution.py:231
  51.2 24.8 %collective-permute-start.6 = (bf16[2,128,256]{2,1,0:T(8,128)(2,1)S(1)}, bf16[2,128,256]{2,1,0:T(8,128)(2,1)S(1)}, u32[]{:S(2)}, u32[]{:S(2)}) collective-permute-start(bf16[2,128,256]{2,1,0:T(8,128)(2,1)S(1)} %slice_reduce_fusion), channel_id=1, source_target_pairs={{0,2},{1,3},{2,0},{3,1},{4,6},{5,7},{6,4},{7,5},{8,10},{9,11},{10,... | collective-permute-start | bytes 393224 | tf_op jit(solution)/shard_map/ppermute | solution.py:26
  65.6 15.8 %collective-permute-start.7 = (bf16[2,128,256]{2,1,0:T(8,128)(2,1)S(1)}, bf16[2,128,256]{2,1,0:T(8,128)(2,1)S(1)}, u32[]{:S(2)}, u32[]{:S(2)}) collective-permute-start(bf16[2,128,256]{2,1,0:T(8,128)(2,1)S(1)} %get-tuple-element.43), channel_id=1, source_target_pairs={{0,1},{1,2},{2,3},{3,0},{4,5},{5,6},{6,7},{7,4},{8,9},{9,10},{10,1... | collective-permute-start | bytes 393224 | tf_op jit(solution)/shard_map/ppermute | solution.py:26
  70.4 16.3 %collective-permute-start.8 = (bf16[2,128,256]{2,1,0:T(8,128)(2,1)S(1)}, bf16[2,128,256]{2,1,0:T(8,128)(2,1)S(1)}, u32[]{:S(2)}, u32[]{:S(2)}) collective-permute-start(bf16[2,128,256]{2,1,0:T(8,128)(2,1)S(1)} %get-tuple-element.44), channel_id=1, source_target_pairs={{0,3},{1,0},{2,1},{3,2},{4,7},{5,4},{6,5},{7,6},{8,11},{9,8},{10,9... | collective-permute-start | bytes 393224 | tf_op jit(solution)/shard_map/ppermute | solution.py:26

commit v3 on v2

v3 whole, which is shorter than its diff:
```python
import functools

import jax
import jax.numpy as jnp
from jax import lax
from jax.experimental import pallas as pl
from jax.experimental.pallas import tpu as pltpu
from jax.sharding import PartitionSpec as P

NV = 200
NC = 300
N_X = 4
N_Z = 4
X_GROUPS = [[x * N_Z + z for x in range(N_X)] for z in range(N_Z)]
F32 = jnp.float32
BF16 = jnp.bfloat16
VMEM_LIMIT = 63 * 2**20
ANY = pl.BlockSpec(memory_space=pl.ANY)
VMEM = pl.BlockSpec(memory_space=pltpu.VMEM)
FIRST_ROWS = (2,)
OTHER_ROWS = (1, 3, 0)


def along_z(x, by):
    pairs = [(a * N_Z + z, a * N_Z + (z + by) % N_Z) for a in range(N_X) for z in range(N_Z)]
    return lax.ppermute(x, "pw", pairs)


def call(kernel, name, out_shape, in_specs, scratch, flops):
    return pl.pallas_call(
        kernel,
        in_specs=in_specs,
        out_specs=jax.tree.map(lambda _: ANY, out_shape),
        out_shape=out_shape,
        scratch_shapes=scratch,
        compiler_params=pltpu.CompilerParams(vmem_limit_bytes=VMEM_LIMIT),
        cost_estimate=pl.CostEstimate(flops=flops, bytes_accessed=10**6, transcendentals=0),
        name=name,
    )


def picked_rows(form, rows):
    hits = lax.broadcasted_iota(jnp.int32, (rows.shape[0], form.shape[0]), 1) == rows
    return jnp.dot(hits.astype(F32).astype(BF16), form, preferred_element_type=F32)


def density(rows_val, rows_cond, val_form, cond_form):
    rows = jnp.concatenate([rows_val, rows_cond] * 4, axis=0).T
    picked = picked_rows(val_form, rows[:, 0:1]) * picked_rows(cond_form, rows[:, 1:2])
    return picked.astype(BF16)


def res_kernel(
    pair_ref, val_ref, cond_ref, bands_ref, out_ref, in_ref, bands, val, cond, pair, dens, sems
):
    rows, groups = pair.shape
    own = rows // (N_X * N_Z)
    pw = lax.axis_index("pw")
    my_x, my_z = pw // N_Z, pw % N_Z
    tables = table_copies((bands_ref, val_ref, cond_ref), (bands, val, cond), sems, 0)
    for copy in tables:
        copy.start()
    read = pltpu.make_async_copy(pair_ref, pair, sems.at[3])
    read.start()
    for copy in tables:
        copy.wait()
    rows_val = bands[2:3, :] * NV + bands[0:1, :]
    rows_cond = bands[2:3, :] * NC + bands[1:2, :]
    dens[...] = density(rows_val, rows_cond, val[...], cond[...])
    read.wait()
    gives = []
    for ref, steps in ((out_ref, FIRST_ROWS), (in_ref, OTHER_ROWS)):
        for x in range(N_X):
            for k, m in enumerate(steps):
                owner_x = x if ref is out_ref else (x + my_x) % N_X
                owner = owner_x * N_Z + (my_z + m) % N_Z
                source = pl.ds(pl.multiple_of(owner * own, own), own)
                target = ref.at[pl.ds((x * len(steps) + k) * own, own), :]
                at = 4 + 2 * len(gives) // 2
                gives.append(
                    pltpu.make_async_copy(
                        pair.at[source, :], target.at[:, pl.ds(0, groups)], sems.at[at]
                    )
                )
                gives.append(
                    pltpu.make_async_copy(
                        dens.at[source, :],
                        target.at[:, pl.ds(groups, dens.shape[1])],
                        sems.at[at + 1],
                    )
                )
    for give in gives:
        give.start()
    for give in gives:
        give.wait()


def table_copies(refs, places, sems, first):
    return [
        pltpu.make_async_copy(ref, place, sems.at[first + k])
        for k, (ref, place) in enumerate(zip(refs, places, strict=True))
    ]


def product(left, right):
    return lax.dot_general(
        left, right, (((1,), (1,)), ((), ())), preferred_element_type=F32
    ).astype(BF16)


def out_kernel(
    left_ref, far_ref, even_ref, from_odd_ref, far_bands_ref, near_bands_ref,
    coulomb_ref, screening_ref, val_ref, cond_ref, out_ref, band_ref, near, far, near_bands,
    far_bands, coulomb, screening, val, cond, left, band, out, sems,
):
    cols, groups = near.shape

    odd = lax.axis_index("blk") % 2

    @pl.when(odd == 0)
    def _():
        pltpu.make_async_copy(from_odd_ref, near, sems.at[0]).start()

    @pl.when(odd != 0)
    def _():
        pltpu.make_async_copy(even_ref, near, sems.at[0]).start()

    refs = (far_ref, coulomb_ref, screening_ref, val_ref, cond_ref)
    copies = table_copies(refs, (far, coulomb, screening, val, cond), sems, 1)
    copies += table_copies((near_bands_ref, far_bands_ref), (near_bands, far_bands), sems, 10)
    for copy in copies:
        copy.start()
    rows = pltpu.make_async_copy(left_ref, left, sems.at[6])
    rows.start()
    pltpu.make_async_copy(from_odd_ref, near, sems.at[0]).wait()
    for copy in copies:
        copy.wait()
    bands = jnp.concatenate([near_bands[...], far_bands[...]], axis=1)
    rows_val = bands[2:3, :] * NV + bands[0:1, :]
    rows_cond = bands[2:3, :] * NC + bands[1:2, :]
    dens = density(rows_val, rows_cond, val[...], cond[...])
    band[:, groups:] = -((dens.astype(F32) * screening[...][None, :]).astype(BF16))
    for k, payload in enumerate((near, far)):
        weighted = (payload[...].astype(F32) * coulomb[...][None, :]).astype(BF16)
        band[k * cols : (k + 1) * cols, :groups] = weighted * 2
    keep = pltpu.make_async_copy(band, band_ref, sems.at[0])
    keep.start()
    rows.wait()
    half = out.shape[0] // 2
    halves = (out_ref.at[pl.ds(0, half)], out_ref.at[pl.ds(half, half)])
    give_product(left, band, out, halves, sems)
    keep.wait()


def give_product(left, band, out, out_refs, sems):
    gives = []
    count, steps, own, cols = out.shape
    each = count // len(out_refs)
    for k, ref in enumerate(out_refs):
        total = product(left[pl.ds(k * each * own, each * own), :], band[...])
        for n in range(each):
            for step in range(steps):
                out[k * each + n, step] = total[
                    n * own : (n + 1) * own, step * cols : (step + 1) * cols
                ]
        gives.append(pltpu.make_async_copy(out.at[pl.ds(k * each, each)], ref, sems.at[1 + k]))
        gives[-1].start()
    for give in gives:
        give.wait()


def in_kernel(
    left_ref, band_ref, out_0, out_1, out_2, out_3, own_ref, left, band, out, sems, out_sems
):
    rows = table_copies((left_ref, band_ref), (left, band), sems, 0)
    for copy in rows:
        copy.start()
    for copy in rows:
        copy.wait()
    my_x = lax.axis_index("pw") // N_Z
    count, steps, own, cols = out.shape
    each = count // N_X
    gives = []
    for by, ref in ((1, out_1), (3, out_3), (2, out_2), (0, out_0)):
        total = product(left[pl.ds(by * each * own, each * own), :], band[...])
        for n in range(each):
            for step in range(steps):
                out[by * each + n, step] = total[
                    n * own : (n + 1) * own, step * cols : (step + 1) * cols
                ]
        owner = own_ref.at[pl.ds((my_x + by) % N_X, 1)]
        gives += [
            pltpu.make_async_copy(
                out.at[pl.ds(by * each, each - 1)], ref, out_sems.at[2 * by]
            ),
            pltpu.make_async_copy(
                out.at[pl.ds(by * each + each - 1, 1)], owner, out_sems.at[2 * by + 1]
            ),
        ]
        gives[-2].start()
        gives[-1].start()
    for give in gives:
        give.wait()


def along_x(x, by):
    pairs = [(a * N_Z + z, (a + by) % N_X * N_Z + z) for a in range(N_X) for z in range(N_Z)]
    return lax.ppermute(x, "pw", pairs)


def taken_kernel(first_ref, second_ref, third_ref, out_ref):
    out_ref[...] = (
        first_ref[...].astype(F32) + second_ref[...].astype(F32) + third_ref[...].astype(F32)
    )


def shares_over_x(pieces):
    return lax.all_to_all(pieces, "pw", 0, 0, axis_index_groups=X_GROUPS)


def local(res_pair, band_pair, coulomb, screening, val_form, cond_form, res_bands, band_bands):
    rows, groups = res_pair.shape
    cols = band_pair.shape[0]
    depth = groups + val_form.shape[1]
    own = rows // (N_X * N_Z)
    few, many = (rows * len(steps) // N_Z for steps in (FIRST_ROWS, OTHER_ROWS))
    blocks = lax.axis_size("blk")
    far_on = [(i, (i + 2) % blocks) for i in range(blocks)]
    far = lax.ppermute(band_pair, "blk", far_on)
    far_bands = lax.ppermute(band_bands, "blk", far_on)
    near_bands = lax.ppermute(band_bands, "blk", [(i, (i + 1) % blocks) for i in range(blocks)])
    from_even = lax.ppermute(band_pair, "blk", [(i, i + 1) for i in range(0, blocks, 2)])

    tables = (coulomb, screening, val_form, cond_form)
    form_scratch = [pltpu.VMEM(t.shape, t.dtype) for t in tables]
    band = pltpu.VMEM((2 * cols, depth), BF16)
    block = pltpu.VMEM(band_pair.shape, BF16)
    index = pltpu.VMEM(band_bands.shape, jnp.int32)
    band_shape = jax.ShapeDtypeStruct((2 * cols, depth), BF16)
    left_out, left_in = call(
        res_kernel,
        "res_rows",
        tuple(jax.ShapeDtypeStruct((n, depth), BF16) for n in (few, many)),
        [ANY] * 4,
        [
            pltpu.VMEM(res_bands.shape, jnp.int32),
            *form_scratch[2:],
            pltpu.VMEM((rows, groups), BF16),
            pltpu.VMEM((rows, depth - groups), BF16),
            pltpu.SemaphoreType.DMA((4 + 4 * N_X * N_Z,)),
        ],
        2 * 10**9,
    )(res_pair, val_form, cond_form, res_bands)
    far, far_bands, near_bands, left_out, left_in, tables = lax.optimization_barrier(
        (far, far_bands, near_bands, left_out, left_in, tables)
    )
    from_odd = lax.ppermute(far, "blk", [(i + 1, i) for i in range(0, blocks, 2)])
    out_term, bands = call(
        out_kernel,
        "out_term",
        (jax.ShapeDtypeStruct((few // own, 2, own, cols), BF16), band_shape),
        [ANY] * 10,
        [
            block,
            block,
            index,
            index,
            *form_scratch,
            pltpu.VMEM((few, depth), BF16),
            band,
            pltpu.VMEM((few // own, 2, own, cols), BF16),
            pltpu.SemaphoreType.DMA((12,)),
        ],
        2 * 10**9,
    )(left_out, far, from_even, from_odd, far_bands, near_bands, *tables)
    *in_terms, own_terms = call(
        in_kernel,
        "in_term",
        (jax.ShapeDtypeStruct((len(OTHER_ROWS) - 1, 2, own, cols), BF16),) * N_X
        + (jax.ShapeDtypeStruct((N_X, 2, own, cols), BF16),),
        [ANY] * 2,
        [
            pltpu.VMEM((many, depth), BF16),
            band,
            pltpu.VMEM((many // own, 2, own, cols), BF16),
            pltpu.SemaphoreType.DMA((2,)),
            pltpu.SemaphoreType.DMA((2 * N_X,)),
        ],
        2 * 10**9,
    )(left_in, bands)

    to_2 = jnp.sum(shares_over_x(out_term).astype(F32), axis=0).astype(BF16)
    from_2 = along_z(to_2, 2)
    own_share, _ = lax.optimization_barrier((in_terms[0], to_2))
    shares = [own_share] + [along_x(in_terms[by], by) for by in (1, 3, 2)]

    def summed(k):
        return sum(s[k].astype(F32) for s in shares)

    to_1, to_3 = summed(0).astype(BF16), summed(1).astype(BF16)
    from_1 = along_z(to_1, 1)
    from_3 = along_z(to_3, 3)
    own_terms, _, _ = lax.optimization_barrier((own_terms, to_1, to_3))
    total = jnp.sum(shares_over_x(own_terms).astype(F32), axis=0)
    taken = pl.pallas_call(
        taken_kernel,
        in_specs=[VMEM] * 3,
        out_specs=VMEM,
        out_shape=jax.ShapeDtypeStruct(from_2.shape, F32),
        compiler_params=pltpu.CompilerParams(vmem_limit_bytes=4 * 2**20),
        cost_estimate=pl.CostEstimate(flops=8000000000, bytes_accessed=10**6, transcendentals=0),
        name="taken",
    )(from_2, from_3, from_1)
    return total + taken


def solution(mesh):
    return jax.shard_map(
        local,
        mesh=mesh,
        in_specs=(
            P("blk", "pw"),
            P("blk", "pw"),
            P("pw"),
            P("pw"),
            P(None, "pw"),
            P(None, "pw"),
            P(None, "blk"),
            P(None, "blk"),
        ),
        out_specs=P(None, ("blk", "pw"), None),
        check_vma=False,
    )
```

time: 88.1 us -> 86.7 us (0.984)
  starting transfers between devices: 51 us -> 57.6 us
  waiting for transfers between devices: 16.6 us -> 12.3 us
  other arithmetic: 4.12 us -> 2 us
  Pallas kernels: 15.6 us -> 14 us
    ppermute x2 -> x4, starting transfers between devices: 5.67 us -> 13.6 us  [the longest x1 4.39 us: local(): lax.ppermute(band_bands, 'blk', [(i, (i + 1) % blocks) for i in range(blo...]
    ppermute x1, starting transfers between devices: 8.43 us -> 3.97 us  [local(): lax.ppermute(far, 'blk', [(i + 1, i) for i in range(0, blocks, 2)])]
    ppermute x2 -> x4, waiting for transfers between devices: 4.02 us -> 0.4 us  [the longest x1 0.39 us: local(): far_bands = lax.ppermute(band_bands, 'blk', far_on)]
    all_to_all x1 -> x2, starting transfers between devices: 4.27 us -> 6.99 us  [shares_over_x(): return lax.all_to_all(pieces, 'pw', 0, 0, axis_index_groups=X_GROUPS)]
    reduce_sum x2, other arithmetic: 2.26 us -> 0.16 us  [the longest x1 0.08 us: local(): to_2 = jnp.sum(shares_over_x(out_term).astype(F32), axis=0).astype(BF16)]
    all_to_all x1 -> x2, waiting for transfers between devices: 1.05 us -> 0.01 us  [shares_over_x(): return lax.all_to_all(pieces, 'pw', 0, 0, axis_index_groups=X_GROUPS)]
    pallas_call x2, Pallas kernels: 5.66 us -> 4.69 us  [the longest x1 4.64 us: local(): call(in_kernel, 'in_term', (jax.ShapeDtypeStruct((len(OTHER_ROWS) - 1, 2,...]
  transfers between devices with their start and end apart: 10 -> 13, of which waited for: 5 -> 3; matrix products, arithmetic and copies ran while one was open for 4% -> 1% of each run, Pallas kernels for 11% -> 12%
where the time goes in v3:
time: 86.7 us; the launch traced here: 86.1 us
  starting transfers between devices  57.6 us (66%)
  Pallas kernels  14 us (16%)
  waiting for transfers between devices  12.3 us (14%)
  other arithmetic  2 us (2%)
    ppermute x3, starting transfers between devices, along_z(): return lax.ppermute(x, 'pw', pairs)  22.9 us
    ppermute x3, waiting for transfers between devices, along_z(): return lax.ppermute(x, 'pw', pairs)  11.2 us
    ppermute x3, starting transfers between devices, along_x(): return lax.ppermute(x, 'pw', pairs)  10.2 us
    all_to_all x2, starting transfers between devices, shares_over_x(): return lax.all_to_all(pieces, 'pw', 0, 0, axis_index_groups=X_GROUPS)  6.99 us
    pallas_call x1, Pallas kernels, local(): call(res_kernel, 'res_rows', tuple((jax.ShapeDtypeStruct((n, depth), BF16...  5.44 us
    pallas_call x1, Pallas kernels, local(): call(in_kernel, 'in_term', (jax.ShapeDtypeStruct((len(OTHER_ROWS) - 1, 2,...  4.64 us
    ppermute x1, starting transfers between devices, local(): lax.ppermute(band_bands, 'blk', [(i, (i + 1) % blocks) for i in range(blo...  4.39 us
    ppermute x1, starting transfers between devices, local(): far = lax.ppermute(band_pair, 'blk', far_on)  4.36 us
  transfers between devices with their start and end apart: 13, of which 3 were waited for; matrix products, arithmetic and copies ran while one was open for 1% of the time, Pallas kernels for 12%

profile of v3, /device:TPU:1, one launch (start us, length us, event | category | flops | bytes accessed | tf_op | source)
XLA Modules:
  0.0 86.1 jit_solution(17840663725559278784)
XLA Ops:
  0.0 4.4 %collective-permute-start = (bf16[256,768]{1,0:T(8,128)(2,1)}, bf16[256,768]{1,0:T(8,128)(2,1)S(1)}, u32[]{:S(2)}, u32[]{:S(2)}) collective-permute-start(bf16[256,768]{1,0:T(8,128)(2,1)} %param.9), channel_id=1, source_target_pairs={{0,32},{16,48},{32,64},{48,80},{64,96},{80,112},{96,128},{112,144}... | collective-permute-start | bytes 1179656 | tf_op jit(solution)/shard_map/ppermute | solution.py:229
  4.4 4.4 %collective-permute-start.2 = (s32[3,256]{1,0:T(4,128)}, s32[3,256]{1,0:T(4,128)S(1)}, u32[]{:S(2)}, u32[]{:S(2)}) collective-permute-start(s32[3,256]{1,0:T(4,128)} %param.15), channel_id=1, source_target_pairs={{0,16},{16,32},{32,48},{48,64},{64,80},{80,96},{96,112},{112,128},... | collective-permute-start | bytes 9224 | tf_op jit(solution)/shard_map/ppermute | solution.py:231
  8.8 3.5 %collective-permute-start.1 = (s32[3,256]{1,0:T(4,128)}, s32[3,256]{1,0:T(4,128)S(1)}, u32[]{:S(2)}, u32[]{:S(2)}) collective-permute-start(s32[3,256]{1,0:T(4,128)} %param.15), channel_id=1, source_target_pairs={{0,32},{16,48},{32,64},{48,80},{64,96},{80,112},{96,128},{112,144}... | collective-permute-start | bytes 9224 | tf_op jit(solution)/shard_map/ppermute | solution.py:230
  12.3 1.3 %collective-permute-start.3 = (bf16[256,768]{1,0:T(8,128)(2,1)}, bf16[256,768]{1,0:T(8,128)(2,1)S(1)}, u32[]{:S(2)}, u32[]{:S(2)}) collective-permute-start(bf16[256,768]{1,0:T(8,128)(2,1)} %param.9), channel_id=1, source_target_pairs={{0,16},{32,48},{64,80},{96,112},{128,144},{160,176},{192,208},{224... | collective-permute-start | bytes 1179656 | tf_op jit(solution)/shard_map/ppermute | solution.py:232
  13.6 5.4 %res_rows.1 = (bf16[512,896]{1,0:T(8,128)(2,1)}, bf16[1536,896]{1,0:T(8,128)(2,1)}) custom-call(bf16[2048,768]{1,0:T(8,128)(2,1)} %pair_ref.1, bf16[400,128]{1,0:T(8,128)(2,1)} %val_ref.2, bf16[600,128]{1,0:T(8,128)(2,1)} %cond_ref.2, s32[3,2048]{1,0:T(4,128)} %bands_ref.1), custom_call_target="tpu_custom_call" | custom-call | flops 2000000000 | bytes 1000000 | tf_op jit(solution)/shard_map/res_rows/pallas_call | solution.py:240
  19.1 0.0 collective-permute-done.2.near_bands_ref
  19.1 0.4 collective-permute-done.1.far_bands_ref
  19.5 0.0 collective-permute-done.far_ref
  19.5 4.0 %collective-permute-start.4 = (bf16[256,768]{1,0:T(8,128)(2,1)S(1)}, bf16[256,768]{1,0:T(8,128)(2,1)}, u32[]{:S(2)}, u32[]{:S(2)}) collective-permute-start(bf16[256,768]{1,0:T(8,128)(2,1)S(1)} %collective-permute-done.far_ref), channel_id=1, source_target_pairs={{16,0},{48,32},{80,64},{112,96},{144,128},{176,160},{208,192},{240... | collective-permute-start | bytes 1179656 | tf_op jit(solution)/shard_map/ppermute | solution.py:257
  23.5 0.0 collective-permute-done.3.even_ref
  23.5 0.7 collective-permute-done.4.from_odd_ref
  24.2 0.0 copy-done.1
  24.2 3.9 %out_term.1 = (bf16[4,2,128,256]{3,2,1,0:T(8,128)(2,1)}, bf16[512,896]{1,0:T(8,128)(2,1)}) custom-call(bf16[512,896]{1,0:T(8,128)(2,1)} %get-tuple-element.28.left_ref, bf16[256,768]{1,0:T(8,128)(2,1)} %copy-done, bf16[256,768]{1,0:T(8,128)(2,1)} %copy-done.1, bf16[256,768]{1,0:T(8,128)(2,1)} %collective-permute-done.4.from_odd_ref, s32[3,256]{1,0:T(4,128)} %copy-done.3, ...), custom_call_target="tpu_custom_call" | custom-call | flops 2000000000 | bytes 1000000 | tf_op jit(solution)/shard_map/out_term/pallas_call | solution.py:258
  28.1 3.5 %all-to-all-start = ((bf16[4,2,128,256]{3,2,1,0:T(8,128)(2,1)}), bf16[4,2,128,256]{3,2,1,0:T(8,128)(2,1)S(1)}, u32[]{:S(2)}, u32[]{:S(2)}) async-start(bf16[4,2,128,256]{3,2,1,0:T(8,128)(2,1)} %get-tuple-element.39), calls=%async_computation | async-start | bytes 1048576 | tf_op jit(solution)/shard_map/all_to_all | solution.py:218
  31.6 4.6 %in_term.1 = (bf16[2,2,128,256]{3,2,1,0:T(8,128)(2,1)}, bf16[2,2,128,256]{3,2,1,0:T(8,128)(2,1)}, bf16[2,2,128,256]{3,2,1,0:T(8,128)(2,1)}, bf16[2,2,128,256]{3,2,1,0:T(8,128)(2,1)}, bf16[4,2,128,256]{3,2,1,0:T(8,128)(2,1)}) custom-call(bf16[1536,896]{1,0:T(8,128)(2,1)} %get-tuple-element.27.left_ref, bf16[512,896]{1,0:T(8,128)(2,1)} %get-tuple-element.36.band_ref), custom_call_target="tpu_custom_call" | custom-call | flops 2000000000 | bytes 1000000 | tf_op jit(solution)/shard_map/in_term/pallas_call | solution.py:276
  36.3 3.4 %collective-permute-start.5 = (bf16[2,2,128,256]{3,2,1,0:T(8,128)(2,1)}, bf16[2,2,128,256]{3,2,1,0:T(8,128)(2,1)S(1)}, u32[]{:S(2)}, u32[]{:S(2)}) collective-permute-start(bf16[2,2,128,256]{3,2,1,0:T(8,128)(2,1)} %get-tuple-element.41), channel_id=1, source_target_pairs={{0,4},{1,5},{2,6},{3,7},{4,8},{5,9},{6,10},{7,11},{8,12},{9,13},{1... | collective-permute-start | bytes 786440 | tf_op jit(solution)/shard_map/ppermute | solution.py:208
  39.6 3.1 %collective-permute-start.6 = (bf16[2,2,128,256]{3,2,1,0:T(8,128)(2,1)}, bf16[2,2,128,256]{3,2,1,0:T(8,128)(2,1)S(1)}, u32[]{:S(2)}, u32[]{:S(2)}) collective-permute-start(bf16[2,2,128,256]{3,2,1,0:T(8,128)(2,1)} %get-tuple-element.42), channel_id=1, source_target_pairs={{0,12},{1,13},{2,14},{3,15},{4,0},{5,1},{6,2},{7,3},{8,4},{9,5},{1... | collective-permute-start | bytes 786440 | tf_op jit(solution)/shard_map/ppermute | solution.py:208
  42.8 3.7 %collective-permute-start.7 = (bf16[2,2,128,256]{3,2,1,0:T(8,128)(2,1)}, bf16[2,2,128,256]{3,2,1,0:T(8,128)(2,1)S(1)}, u32[]{:S(2)}, u32[]{:S(2)}) collective-permute-start(bf16[2,2,128,256]{3,2,1,0:T(8,128)(2,1)} %get-tuple-element.43), channel_id=1, source_target_pairs={{0,8},{1,9},{2,10},{3,11},{4,12},{5,13},{6,14},{7,15},{8,0},{9,1},... | collective-permute-start | bytes 786440 | tf_op jit(solution)/shard_map/ppermute | solution.py:208
  46.4 0.0 all-to-all-done
  46.4 0.1 reduce_sum.21
  46.5 13.7 %collective-permute-start.8 = (bf16[2,128,256]{2,1,0:T(8,128)(2,1)S(1)}, bf16[2,128,256]{2,1,0:T(8,128)(2,1)S(1)}, u32[]{:S(2)}, u32[]{:S(2)}) collective-permute-start(bf16[2,128,256]{2,1,0:T(8,128)(2,1)S(1)} %reduce_sum.21), channel_id=1, source_target_pairs={{0,2},{1,3},{2,0},{3,1},{4,6},{5,7},{6,4},{7,5},{8,10},{9,11},{10,... | collective-permute-start | bytes 393224 | tf_op jit(solution)/shard_map/ppermute | solution.py:26
  60.2 0.0 collective-permute-done.5
  60.2 0.0 collective-permute-done.7
  60.2 1.1 %fusion.1 = (bf16[2,128,256]{2,1,0:T(8,128)(2,1)S(1)}, bf16[2,128,256]{2,1,0:T(8,128)(2,1)S(1)}) fusion(bf16[2,2,128,256]{3,2,1,0:T(8,128)(2,1)S(1)} %collective-permute-done.7, bf16[2,2,128,256]{3,2,1,0:T(8,128)(2,1)S(1)} %collective-permute-done.6, bf16[2,2,128,256]{3,2,1,0:T(8,128)(2,1)S(1)} %collective-permute-done.5, ...), kind=kLoop, calls=%fused_computation.4 | loop fusion | flops 1048576 | bytes 1310720 | tf_op jit(solution)/shard_map/add | solution.py:298
  61.3 3.4 %collective-permute-start.9 = (bf16[2,128,256]{2,1,0:T(8,128)(2,1)S(1)}, bf16[2,128,256]{2,1,0:T(8,128)(2,1)S(1)}, u32[]{:S(2)}, u32[]{:S(2)}) collective-permute-start(bf16[2,128,256]{2,1,0:T(8,128)(2,1)S(1)} %get-tuple-element.45), channel_id=1, source_target_pairs={{0,3},{1,0},{2,1},{3,2},{4,7},{5,4},{6,5},{7,6},{8,11},{9,8},{10,9... | collective-permute-start | bytes 393224 | tf_op jit(solution)/shard_map/ppermute | solution.py:26
  64.8 5.8 %collective-permute-start.10 = (bf16[2,128,256]{2,1,0:T(8,128)(2,1)S(1)}, bf16[2,128,256]{2,1,0:T(8,128)(2,1)S(1)}, u32[]{:S(2)}, u32[]{:S(2)}) collective-permute-start(bf16[2,128,256]{2,1,0:T(8,128)(2,1)S(1)} %get-tuple-element.46), channel_id=1, source_target_pairs={{0,1},{1,2},{2,3},{3,0},{4,5},{5,6},{6,7},{7,4},{8,9},{9,10},{10,1... | collective-permute-start | bytes 393224 | tf_op jit(solution)/shard_map/ppermute | solution.py:26
  70.5 3.5 %all-to-all-start.1 = ((bf16[4,2,128,256]{3,2,1,0:T(8,128)(2,1)}), bf16[4,2,128,256]{3,2,1,0:T(8,128)(2,1)S(1)}, u32[]{:S(2)}, u32[]{:S(2)}) async-start(bf16[4,2,128,256]{3,2,1,0:T(8,128)(2,1)} %get-tuple-element.44), calls=%async_computation.1 | async-start | bytes 1048576 | tf_op jit(solution)/shard_map/all_to_all | solution.py:218
  74.0 0.0 collective-permute-done.8.first_ref
  74.0 11.2 %collective-permute-done.9.second_ref = bf16[2,128,256]{2,1,0:T(8,128)(2,1)S(1)} collective-permute-done((bf16[2,128,256]{2,1,0:T(8,128)(2,1)S(1)}, bf16[2,128,256]{2,1,0:T(8,128)(2,1)S(1)}, u32[]{:S(2)}, u32[]{:S(2)}) %collective-permute-start.9) | collective-permute-done | bytes 131104 | tf_op jit(solution)/shard_map/ppermute | solution.py:26
  85.3 0.0 collective-permute-done.10.third_ref
  85.3 0.1 convert_reduce_fusion
  85.4 0.7 add.39
  (10 shorter events, 0.1 us)
Async XLA Ops:
  0.0 19.5 %collective-permute-start = (bf16[256,768]{1,0:T(8,128)(2,1)}, bf16[256,768]{1,0:T(8,128)(2,1)S(1)}, u32[]{:S(2)}, u32[]{:S(2)}) collective-permute-start(bf16[256,768]{1,0:T(8,128)(2,1)} %param.9), channel_id=1, source_target_pairs={{0,32},{16,48},{32,64},{48,80},{64,96},{80,112},{96,128},{112,144}... | collective-permute-start | bytes 1179656 | tf_op jit(solution)/shard_map/ppermute | solution.py:229
  4.4 14.7 %collective-permute-start.2 = (s32[3,256]{1,0:T(4,128)}, s32[3,256]{1,0:T(4,128)S(1)}, u32[]{:S(2)}, u32[]{:S(2)}) collective-permute-start(s32[3,256]{1,0:T(4,128)} %param.15), channel_id=1, source_target_pairs={{0,16},{16,32},{32,48},{48,64},{64,80},{80,96},{96,112},{112,128},... | collective-permute-start | bytes 9224 | tf_op jit(solution)/shard_map/ppermute | solution.py:231
  8.8 10.7 %collective-permute-start.1 = (s32[3,256]{1,0:T(4,128)}, s32[3,256]{1,0:T(4,128)S(1)}, u32[]{:S(2)}, u32[]{:S(2)}) collective-permute-start(s32[3,256]{1,0:T(4,128)} %param.15), channel_id=1, source_target_pairs={{0,32},{16,48},{32,64},{48,80},{64,96},{80,112},{96,128},{112,144}... | collective-permute-start | bytes 9224 | tf_op jit(solution)/shard_map/ppermute | solution.py:230
  12.3 11.1 %collective-permute-start.3 = (bf16[256,768]{1,0:T(8,128)(2,1)}, bf16[256,768]{1,0:T(8,128)(2,1)S(1)}, u32[]{:S(2)}, u32[]{:S(2)}) collective-permute-start(bf16[256,768]{1,0:T(8,128)(2,1)} %param.9), channel_id=1, source_target_pairs={{0,16},{32,48},{64,80},{96,112},{128,144},{160,176},{192,208},{224... | collective-permute-start | bytes 1179656 | tf_op jit(solution)/shard_map/ppermute | solution.py:232
  19.1 5.1 %copy-start.2 = (s32[3,256]{1,0:T(4,128)}, s32[3,256]{1,0:T(4,128)S(1)}, u32[]{:S(2)}) copy-start(s32[3,256]{1,0:T(4,128)S(1)} %collective-permute-done.2.near_bands_ref) | copy-start | bytes 9220
  19.5 4.7 %copy-start.3 = (s32[3,256]{1,0:T(4,128)}, s32[3,256]{1,0:T(4,128)S(1)}, u32[]{:S(2)}) copy-start(s32[3,256]{1,0:T(4,128)S(1)} %collective-permute-done.1.far_bands_ref) | copy-start | bytes 9220
  19.5 4.7 %copy-start = (bf16[256,768]{1,0:T(8,128)(2,1)}, bf16[256,768]{1,0:T(8,128)(2,1)S(1)}, u32[]{:S(2)}) copy-start(bf16[256,768]{1,0:T(8,128)(2,1)S(1)} %collective-permute-done.far_ref) | copy-start | bytes 1179652
  19.5 4.7 %collective-permute-start.4 = (bf16[256,768]{1,0:T(8,128)(2,1)S(1)}, bf16[256,768]{1,0:T(8,128)(2,1)}, u32[]{:S(2)}, u32[]{:S(2)}) collective-permute-start(bf16[256,768]{1,0:T(8,128)(2,1)S(1)} %collective-permute-done.far_ref), channel_id=1, source_target_pairs={{16,0},{48,32},{80,64},{112,96},{144,128},{176,160},{208,192},{240... | collective-permute-start | bytes 1179656 | tf_op jit(solution)/shard_map/ppermute | solution.py:257
  23.5 0.7 copy-start.1
  28.1 18.3 %all-to-all-start = ((bf16[4,2,128,256]{3,2,1,0:T(8,128)(2,1)}), bf16[4,2,128,256]{3,2,1,0:T(8,128)(2,1)S(1)}, u32[]{:S(2)}, u32[]{:S(2)}) async-start(bf16[4,2,128,256]{3,2,1,0:T(8,128)(2,1)} %get-tuple-element.39), calls=%async_computation | async-start | bytes 1048576 | tf_op jit(solution)/shard_map/all_to_all | solution.py:218
  36.3 24.0 %collective-permute-start.5 = (bf16[2,2,128,256]{3,2,1,0:T(8,128)(2,1)}, bf16[2,2,128,256]{3,2,1,0:T(8,128)(2,1)S(1)}, u32[]{:S(2)}, u32[]{:S(2)}) collective-permute-start(bf16[2,2,128,256]{3,2,1,0:T(8,128)(2,1)} %get-tuple-element.41), channel_id=1, source_target_pairs={{0,4},{1,5},{2,6},{3,7},{4,8},{5,9},{6,10},{7,11},{8,12},{9,13},{1... | collective-permute-start | bytes 786440 | tf_op jit(solution)/shard_map/ppermute | solution.py:208
  39.6 20.6 %collective-permute-start.6 = (bf16[2,2,128,256]{3,2,1,0:T(8,128)(2,1)}, bf16[2,2,128,256]{3,2,1,0:T(8,128)(2,1)S(1)}, u32[]{:S(2)}, u32[]{:S(2)}) collective-permute-start(bf16[2,2,128,256]{3,2,1,0:T(8,128)(2,1)} %get-tuple-element.42), channel_id=1, source_target_pairs={{0,12},{1,13},{2,14},{3,15},{4,0},{5,1},{6,2},{7,3},{8,4},{9,5},{1... | collective-permute-start | bytes 786440 | tf_op jit(solution)/shard_map/ppermute | solution.py:208
  42.8 17.5 %collective-permute-start.7 = (bf16[2,2,128,256]{3,2,1,0:T(8,128)(2,1)}, bf16[2,2,128,256]{3,2,1,0:T(8,128)(2,1)S(1)}, u32[]{:S(2)}, u32[]{:S(2)}) collective-permute-start(bf16[2,2,128,256]{3,2,1,0:T(8,128)(2,1)} %get-tuple-element.43), channel_id=1, source_target_pairs={{0,8},{1,9},{2,10},{3,11},{4,12},{5,13},{6,14},{7,15},{8,0},{9,1},... | collective-permute-start | bytes 786440 | tf_op jit(solution)/shard_map/ppermute | solution.py:208
  46.5 27.5 %collective-permute-start.8 = (bf16[2,128,256]{2,1,0:T(8,128)(2,1)S(1)}, bf16[2,128,256]{2,1,0:T(8,128)(2,1)S(1)}, u32[]{:S(2)}, u32[]{:S(2)}) collective-permute-start(bf16[2,128,256]{2,1,0:T(8,128)(2,1)S(1)} %reduce_sum.21), channel_id=1, source_target_pairs={{0,2},{1,3},{2,0},{3,1},{4,6},{5,7},{6,4},{7,5},{8,10},{9,11},{10,... | collective-permute-start | bytes 393224 | tf_op jit(solution)/shard_map/ppermute | solution.py:26
  61.3 23.9 %collective-permute-start.9 = (bf16[2,128,256]{2,1,0:T(8,128)(2,1)S(1)}, bf16[2,128,256]{2,1,0:T(8,128)(2,1)S(1)}, u32[]{:S(2)}, u32[]{:S(2)}) collective-permute-start(bf16[2,128,256]{2,1,0:T(8,128)(2,1)S(1)} %get-tuple-element.45), channel_id=1, source_target_pairs={{0,3},{1,0},{2,1},{3,2},{4,7},{5,4},{6,5},{7,6},{8,11},{9,8},{10,9... | collective-permute-start | bytes 393224 | tf_op jit(solution)/shard_map/ppermute | solution.py:26
  64.8 20.5 %collective-permute-start.10 = (bf16[2,128,256]{2,1,0:T(8,128)(2,1)S(1)}, bf16[2,128,256]{2,1,0:T(8,128)(2,1)S(1)}, u32[]{:S(2)}, u32[]{:S(2)}) collective-permute-start(bf16[2,128,256]{2,1,0:T(8,128)(2,1)S(1)} %get-tuple-element.46), channel_id=1, source_target_pairs={{0,1},{1,2},{2,3},{3,0},{4,5},{5,6},{6,7},{7,4},{8,9},{9,10},{10,1... | collective-permute-start | bytes 393224 | tf_op jit(solution)/shard_map/ppermute | solution.py:26
  70.5 14.8 %all-to-all-start.1 = ((bf16[4,2,128,256]{3,2,1,0:T(8,128)(2,1)}), bf16[4,2,128,256]{3,2,1,0:T(8,128)(2,1)S(1)}, u32[]{:S(2)}, u32[]{:S(2)}) async-start(bf16[4,2,128,256]{3,2,1,0:T(8,128)(2,1)} %get-tuple-element.44), calls=%async_computation.1 | async-start | bytes 1048576 | tf_op jit(solution)/shard_map/all_to_all | solution.py:218

commit v4 on v3

--- a/solution.py
+++ b/solution.py
@@ -66,9 +66,11 @@
         copy.wait()
     rows_val = bands[2:3, :] * NV + bands[0:1, :]
     rows_cond = bands[2:3, :] * NC + bands[1:2, :]
-    dens[...] = density(rows_val, rows_cond, val[...], cond[...])
+    half = rows // 2
+    dens[:half, :] = density(rows_val[:, :half], rows_cond[:, :half], val[...], cond[...])
     read.wait()
     gives = []
+    later = []
     for ref, steps in ((out_ref, FIRST_ROWS), (in_ref, OTHER_ROWS)):
         for x in range(N_X):
             for k, m in enumerate(steps):
@@ -76,22 +78,24 @@
                 owner = owner_x * N_Z + (my_z + m) % N_Z
                 source = pl.ds(pl.multiple_of(owner * own, own), own)
                 target = ref.at[pl.ds((x * len(steps) + k) * own, own), :]
-                at = 4 + 2 * len(gives) // 2
+                at = 4 + 2 * len(gives)
                 gives.append(
                     pltpu.make_async_copy(
                         pair.at[source, :], target.at[:, pl.ds(0, groups)], sems.at[at]
                     )
                 )
-                gives.append(
+                gives[-1].start()
+                later.append(
                     pltpu.make_async_copy(
                         dens.at[source, :],
                         target.at[:, pl.ds(groups, dens.shape[1])],
                         sems.at[at + 1],
                     )
                 )
-    for give in gives:
+    dens[half:, :] = density(rows_val[:, half:], rows_cond[:, half:], val[...], cond[...])
+    for give in later:
         give.start()
-    for give in gives:
+    for give in gives + later:
         give.wait()
 
 
@@ -251,8 +255,8 @@
         ],
         2 * 10**9,
     )(res_pair, val_form, cond_form, res_bands)
-    far, far_bands, near_bands, left_out, left_in, tables = lax.optimization_barrier(
-        (far, far_bands, near_bands, left_out, left_in, tables)
+    far, far_bands, near_bands, from_even, left_out, left_in, tables = lax.optimization_barrier(
+        (far, far_bands, near_bands, from_even, left_out, left_in, tables)
     )
     from_odd = lax.ppermute(far, "blk", [(i + 1, i) for i in range(0, blocks, 2)])
     out_term, bands = call(

time: 86.7 us -> 85 us (0.980)
  waiting for transfers between devices: 12.3 us -> 10.5 us
    ppermute x3, waiting for transfers between devices: 11.2 us -> 8.2 us  [along_z(): return lax.ppermute(x, 'pw', pairs)]
    ppermute x1, waiting for transfers between devices: 0.39 us -> 1.62 us  [local(): far_bands = lax.ppermute(band_bands, 'blk', far_on)]
where the time goes in v4:
time: 85 us; the launch traced here: 84.4 us
  starting transfers between devices  58 us (68%)
  Pallas kernels  13.7 us (16%)
  waiting for transfers between devices  10.5 us (12%)
  other arithmetic  2 us (2%)
    ppermute x3, starting transfers between devices, along_z(): return lax.ppermute(x, 'pw', pairs)  22.9 us
    ppermute x3, starting transfers between devices, along_x(): return lax.ppermute(x, 'pw', pairs)  10.1 us
    ppermute x3, waiting for transfers between devices, along_z(): return lax.ppermute(x, 'pw', pairs)  8.2 us
    all_to_all x2, starting transfers between devices, shares_over_x(): return lax.all_to_all(pieces, 'pw', 0, 0, axis_index_groups=X_GROUPS)  6.96 us
    pallas_call x1, Pallas kernels, local(): call(res_kernel, 'res_rows', tuple((jax.ShapeDtypeStruct((n, depth), BF16...  5.07 us
    ppermute x1, starting transfers between devices, local(): lax.ppermute(band_bands, 'blk', [(i, (i + 1) % blocks) for i in range(blo...  4.86 us
    pallas_call x1, Pallas kernels, local(): call(in_kernel, 'in_term', (jax.ShapeDtypeStruct((len(OTHER_ROWS) - 1, 2,...  4.65 us
    ppermute x1, starting transfers between devices, local(): far = lax.ppermute(band_pair, 'blk', far_on)  4.37 us
  transfers between devices with their start and end apart: 13, of which 3 were waited for; matrix products, arithmetic and copies ran while one was open for 1% of the time, Pallas kernels for 12%

profile of v4, /device:TPU:1, one launch (start us, length us, event | category | flops | bytes accessed | tf_op | source)
XLA Modules:
  0.0 84.4 jit_solution(7942035765882306797)
XLA Ops:
  0.0 1.3 %collective-permute-start.3 = (bf16[256,768]{1,0:T(8,128)(2,1)}, bf16[256,768]{1,0:T(8,128)(2,1)S(1)}, u32[]{:S(2)}, u32[]{:S(2)}) collective-permute-start(bf16[256,768]{1,0:T(8,128)(2,1)} %param.9), channel_id=1, source_target_pairs={{0,16},{32,48},{64,80},{96,112},{128,144},{160,176},{192,208},{224... | collective-permute-start | bytes 1179656 | tf_op jit(solution)/shard_map/ppermute | solution.py:236
  1.3 4.4 %collective-permute-start = (bf16[256,768]{1,0:T(8,128)(2,1)}, bf16[256,768]{1,0:T(8,128)(2,1)S(1)}, u32[]{:S(2)}, u32[]{:S(2)}) collective-permute-start(bf16[256,768]{1,0:T(8,128)(2,1)} %param.9), channel_id=1, source_target_pairs={{0,32},{16,48},{32,64},{48,80},{64,96},{80,112},{96,128},{112,144}... | collective-permute-start | bytes 1179656 | tf_op jit(solution)/shard_map/ppermute | solution.py:233
  5.7 4.9 %collective-permute-start.2 = (s32[3,256]{1,0:T(4,128)}, s32[3,256]{1,0:T(4,128)S(1)}, u32[]{:S(2)}, u32[]{:S(2)}) collective-permute-start(s32[3,256]{1,0:T(4,128)} %param.15), channel_id=1, source_target_pairs={{0,16},{16,32},{32,48},{48,64},{64,80},{80,96},{96,112},{112,128},... | collective-permute-start | bytes 9224 | tf_op jit(solution)/shard_map/ppermute | solution.py:235
  10.5 3.5 %collective-permute-start.1 = (s32[3,256]{1,0:T(4,128)}, s32[3,256]{1,0:T(4,128)S(1)}, u32[]{:S(2)}, u32[]{:S(2)}) collective-permute-start(s32[3,256]{1,0:T(4,128)} %param.15), channel_id=1, source_target_pairs={{0,32},{16,48},{32,64},{48,80},{64,96},{80,112},{96,128},{112,144}... | collective-permute-start | bytes 9224 | tf_op jit(solution)/shard_map/ppermute | solution.py:234
  14.1 5.1 %res_rows.1 = (bf16[512,896]{1,0:T(8,128)(2,1)}, bf16[1536,896]{1,0:T(8,128)(2,1)}) custom-call(bf16[2048,768]{1,0:T(8,128)(2,1)} %pair_ref.1, bf16[400,128]{1,0:T(8,128)(2,1)} %val_ref.2, bf16[600,128]{1,0:T(8,128)(2,1)} %cond_ref.2, s32[3,2048]{1,0:T(4,128)} %bands_ref.1), custom_call_target="tpu_custom_call" | custom-call | flops 2000000000 | bytes 1000000 | tf_op jit(solution)/shard_map/res_rows/pallas_call | solution.py:244
  19.2 0.0 collective-permute-done.2.near_bands_ref
  19.2 1.6 %collective-permute-done.1.far_bands_ref = s32[3,256]{1,0:T(4,128)S(1)} collective-permute-done((s32[3,256]{1,0:T(4,128)}, s32[3,256]{1,0:T(4,128)S(1)}, u32[]{:S(2)}, u32[]{:S(2)}) %collective-permute-start.1) | collective-permute-done | bytes 3104 | tf_op jit(solution)/shard_map/ppermute | solution.py:234
  20.8 0.0 collective-permute-done.3.even_ref
  20.8 0.0 collective-permute-done.far_ref
  20.8 4.0 %collective-permute-start.4 = (bf16[256,768]{1,0:T(8,128)(2,1)S(1)}, bf16[256,768]{1,0:T(8,128)(2,1)}, u32[]{:S(2)}, u32[]{:S(2)}) collective-permute-start(bf16[256,768]{1,0:T(8,128)(2,1)S(1)} %collective-permute-done.far_ref), channel_id=1, source_target_pairs={{16,0},{48,32},{80,64},{112,96},{144,128},{176,160},{208,192},{240... | collective-permute-start | bytes 1179656 | tf_op jit(solution)/shard_map/ppermute | solution.py:261
  24.8 0.7 collective-permute-done.4.from_odd_ref
  25.5 3.9 %out_term.1 = (bf16[4,2,128,256]{3,2,1,0:T(8,128)(2,1)}, bf16[512,896]{1,0:T(8,128)(2,1)}) custom-call(bf16[512,896]{1,0:T(8,128)(2,1)} %get-tuple-element.29.left_ref, bf16[256,768]{1,0:T(8,128)(2,1)} %copy-done.1, bf16[256,768]{1,0:T(8,128)(2,1)} %copy-done, bf16[256,768]{1,0:T(8,128)(2,1)} %collective-permute-done.4.from_odd_ref, s32[3,256]{1,0:T(4,128)} %copy-done.3, ...), custom_call_target="tpu_custom_call" | custom-call | flops 2000000000 | bytes 1000000 | tf_op jit(solution)/shard_map/out_term/pallas_call | solution.py:262
  29.4 3.5 %all-to-all-start = ((bf16[4,2,128,256]{3,2,1,0:T(8,128)(2,1)}), bf16[4,2,128,256]{3,2,1,0:T(8,128)(2,1)S(1)}, u32[]{:S(2)}, u32[]{:S(2)}) async-start(bf16[4,2,128,256]{3,2,1,0:T(8,128)(2,1)} %get-tuple-element.41), calls=%async_computation | async-start | bytes 1048576 | tf_op jit(solution)/shard_map/all_to_all | solution.py:222
  32.9 4.7 %in_term.1 = (bf16[2,2,128,256]{3,2,1,0:T(8,128)(2,1)}, bf16[2,2,128,256]{3,2,1,0:T(8,128)(2,1)}, bf16[2,2,128,256]{3,2,1,0:T(8,128)(2,1)}, bf16[2,2,128,256]{3,2,1,0:T(8,128)(2,1)}, bf16[4,2,128,256]{3,2,1,0:T(8,128)(2,1)}) custom-call(bf16[1536,896]{1,0:T(8,128)(2,1)} %get-tuple-element.28.left_ref, bf16[512,896]{1,0:T(8,128)(2,1)} %get-tuple-element.38.band_ref), custom_call_target="tpu_custom_call" | custom-call | flops 2000000000 | bytes 1000000 | tf_op jit(solution)/shard_map/in_term/pallas_call | solution.py:280
  37.6 3.3 %collective-permute-start.5 = (bf16[2,2,128,256]{3,2,1,0:T(8,128)(2,1)}, bf16[2,2,128,256]{3,2,1,0:T(8,128)(2,1)S(1)}, u32[]{:S(2)}, u32[]{:S(2)}) collective-permute-start(bf16[2,2,128,256]{3,2,1,0:T(8,128)(2,1)} %get-tuple-element.43), channel_id=1, source_target_pairs={{0,4},{1,5},{2,6},{3,7},{4,8},{5,9},{6,10},{7,11},{8,12},{9,13},{1... | collective-permute-start | bytes 786440 | tf_op jit(solution)/shard_map/ppermute | solution.py:212
  40.9 3.2 %collective-permute-start.6 = (bf16[2,2,128,256]{3,2,1,0:T(8,128)(2,1)}, bf16[2,2,128,256]{3,2,1,0:T(8,128)(2,1)S(1)}, u32[]{:S(2)}, u32[]{:S(2)}) collective-permute-start(bf16[2,2,128,256]{3,2,1,0:T(8,128)(2,1)} %get-tuple-element.44), channel_id=1, source_target_pairs={{0,12},{1,13},{2,14},{3,15},{4,0},{5,1},{6,2},{7,3},{8,4},{9,5},{1... | collective-permute-start | bytes 786440 | tf_op jit(solution)/shard_map/ppermute | solution.py:212
  44.1 3.6 %collective-permute-start.7 = (bf16[2,2,128,256]{3,2,1,0:T(8,128)(2,1)}, bf16[2,2,128,256]{3,2,1,0:T(8,128)(2,1)S(1)}, u32[]{:S(2)}, u32[]{:S(2)}) collective-permute-start(bf16[2,2,128,256]{3,2,1,0:T(8,128)(2,1)} %get-tuple-element.45), channel_id=1, source_target_pairs={{0,8},{1,9},{2,10},{3,11},{4,12},{5,13},{6,14},{7,15},{8,0},{9,1},... | collective-permute-start | bytes 786440 | tf_op jit(solution)/shard_map/ppermute | solution.py:212
  47.7 0.0 all-to-all-done
  47.7 0.1 reduce_sum.21
  47.8 13.7 %collective-permute-start.8 = (bf16[2,128,256]{2,1,0:T(8,128)(2,1)S(1)}, bf16[2,128,256]{2,1,0:T(8,128)(2,1)S(1)}, u32[]{:S(2)}, u32[]{:S(2)}) collective-permute-start(bf16[2,128,256]{2,1,0:T(8,128)(2,1)S(1)} %reduce_sum.21), channel_id=1, source_target_pairs={{0,2},{1,3},{2,0},{3,1},{4,6},{5,7},{6,4},{7,5},{8,10},{9,11},{10,... | collective-permute-start | bytes 393224 | tf_op jit(solution)/shard_map/ppermute | solution.py:26
  61.5 0.0 collective-permute-done.5
  61.5 0.0 collective-permute-done.6
  61.5 0.0 collective-permute-done.7
  61.5 1.1 %fusion.1 = (bf16[2,128,256]{2,1,0:T(8,128)(2,1)S(1)}, bf16[2,128,256]{2,1,0:T(8,128)(2,1)S(1)}) fusion(bf16[2,2,128,256]{3,2,1,0:T(8,128)(2,1)S(1)} %collective-permute-done.7, bf16[2,2,128,256]{3,2,1,0:T(8,128)(2,1)S(1)} %collective-permute-done.6, bf16[2,2,128,256]{3,2,1,0:T(8,128)(2,1)S(1)} %collective-permute-done.5, ...), kind=kLoop, calls=%fused_computation.4 | loop fusion | flops 1048576 | bytes 1310720 | tf_op jit(solution)/shard_map/add | solution.py:302
  62.7 3.4 %collective-permute-start.9 = (bf16[2,128,256]{2,1,0:T(8,128)(2,1)S(1)}, bf16[2,128,256]{2,1,0:T(8,128)(2,1)S(1)}, u32[]{:S(2)}, u32[]{:S(2)}) collective-permute-start(bf16[2,128,256]{2,1,0:T(8,128)(2,1)S(1)} %get-tuple-element.47), channel_id=1, source_target_pairs={{0,3},{1,0},{2,1},{3,2},{4,7},{5,4},{6,5},{7,6},{8,11},{9,8},{10,9... | collective-permute-start | bytes 393224 | tf_op jit(solution)/shard_map/ppermute | solution.py:26
  66.0 5.8 %collective-permute-start.10 = (bf16[2,128,256]{2,1,0:T(8,128)(2,1)S(1)}, bf16[2,128,256]{2,1,0:T(8,128)(2,1)S(1)}, u32[]{:S(2)}, u32[]{:S(2)}) collective-permute-start(bf16[2,128,256]{2,1,0:T(8,128)(2,1)S(1)} %get-tuple-element.48), channel_id=1, source_target_pairs={{0,1},{1,2},{2,3},{3,0},{4,5},{5,6},{6,7},{7,4},{8,9},{9,10},{10,1... | collective-permute-start | bytes 393224 | tf_op jit(solution)/shard_map/ppermute | solution.py:26
  71.9 3.5 %all-to-all-start.1 = ((bf16[4,2,128,256]{3,2,1,0:T(8,128)(2,1)}), bf16[4,2,128,256]{3,2,1,0:T(8,128)(2,1)S(1)}, u32[]{:S(2)}, u32[]{:S(2)}) async-start(bf16[4,2,128,256]{3,2,1,0:T(8,128)(2,1)} %get-tuple-element.46), calls=%async_computation.1 | async-start | bytes 1048576 | tf_op jit(solution)/shard_map/all_to_all | solution.py:222
  75.4 0.0 collective-permute-done.8.first_ref
  75.4 8.2 %collective-permute-done.9.second_ref = bf16[2,128,256]{2,1,0:T(8,128)(2,1)S(1)} collective-permute-done((bf16[2,128,256]{2,1,0:T(8,128)(2,1)S(1)}, bf16[2,128,256]{2,1,0:T(8,128)(2,1)S(1)}, u32[]{:S(2)}, u32[]{:S(2)}) %collective-permute-start.9) | collective-permute-done | bytes 131104 | tf_op jit(solution)/shard_map/ppermute | solution.py:26
  83.6 0.0 collective-permute-done.10.third_ref
  83.6 0.1 convert_reduce_fusion
  83.7 0.7 add.39
  (10 shorter events, 0.1 us)
Async XLA Ops:
  0.0 20.8 %collective-permute-start.3 = (bf16[256,768]{1,0:T(8,128)(2,1)}, bf16[256,768]{1,0:T(8,128)(2,1)S(1)}, u32[]{:S(2)}, u32[]{:S(2)}) collective-permute-start(bf16[256,768]{1,0:T(8,128)(2,1)} %param.9), channel_id=1, source_target_pairs={{0,16},{32,48},{64,80},{96,112},{128,144},{160,176},{192,208},{224... | collective-permute-start | bytes 1179656 | tf_op jit(solution)/shard_map/ppermute | solution.py:236
  1.3 19.5 %collective-permute-start = (bf16[256,768]{1,0:T(8,128)(2,1)}, bf16[256,768]{1,0:T(8,128)(2,1)S(1)}, u32[]{:S(2)}, u32[]{:S(2)}) collective-permute-start(bf16[256,768]{1,0:T(8,128)(2,1)} %param.9), channel_id=1, source_target_pairs={{0,32},{16,48},{32,64},{48,80},{64,96},{80,112},{96,128},{112,144}... | collective-permute-start | bytes 1179656 | tf_op jit(solution)/shard_map/ppermute | solution.py:233
  5.7 13.5 %collective-permute-start.2 = (s32[3,256]{1,0:T(4,128)}, s32[3,256]{1,0:T(4,128)S(1)}, u32[]{:S(2)}, u32[]{:S(2)}) collective-permute-start(s32[3,256]{1,0:T(4,128)} %param.15), channel_id=1, source_target_pairs={{0,16},{16,32},{32,48},{48,64},{64,80},{80,96},{96,112},{112,128},... | collective-permute-start | bytes 9224 | tf_op jit(solution)/shard_map/ppermute | solution.py:235
  10.5 10.3 %collective-permute-start.1 = (s32[3,256]{1,0:T(4,128)}, s32[3,256]{1,0:T(4,128)S(1)}, u32[]{:S(2)}, u32[]{:S(2)}) collective-permute-start(s32[3,256]{1,0:T(4,128)} %param.15), channel_id=1, source_target_pairs={{0,32},{16,48},{32,64},{48,80},{64,96},{80,112},{96,128},{112,144}... | collective-permute-start | bytes 9224 | tf_op jit(solution)/shard_map/ppermute | solution.py:234
  19.2 6.3 %copy-start.2 = (s32[3,256]{1,0:T(4,128)}, s32[3,256]{1,0:T(4,128)S(1)}, u32[]{:S(2)}) copy-start(s32[3,256]{1,0:T(4,128)S(1)} %collective-permute-done.2.near_bands_ref) | copy-start | bytes 9220
  20.8 4.7 %copy-start.3 = (s32[3,256]{1,0:T(4,128)}, s32[3,256]{1,0:T(4,128)S(1)}, u32[]{:S(2)}) copy-start(s32[3,256]{1,0:T(4,128)S(1)} %collective-permute-done.1.far_bands_ref) | copy-start | bytes 9220
  20.8 4.7 %copy-start = (bf16[256,768]{1,0:T(8,128)(2,1)}, bf16[256,768]{1,0:T(8,128)(2,1)S(1)}, u32[]{:S(2)}) copy-start(bf16[256,768]{1,0:T(8,128)(2,1)S(1)} %collective-permute-done.3.even_ref) | copy-start | bytes 1179652
  20.8 4.7 %copy-start.1 = (bf16[256,768]{1,0:T(8,128)(2,1)}, bf16[256,768]{1,0:T(8,128)(2,1)S(1)}, u32[]{:S(2)}) copy-start(bf16[256,768]{1,0:T(8,128)(2,1)S(1)} %collective-permute-done.far_ref) | copy-start | bytes 1179652
  20.8 4.7 %collective-permute-start.4 = (bf16[256,768]{1,0:T(8,128)(2,1)S(1)}, bf16[256,768]{1,0:T(8,128)(2,1)}, u32[]{:S(2)}, u32[]{:S(2)}) collective-permute-start(bf16[256,768]{1,0:T(8,128)(2,1)S(1)} %collective-permute-done.far_ref), channel_id=1, source_target_pairs={{16,0},{48,32},{80,64},{112,96},{144,128},{176,160},{208,192},{240... | collective-permute-start | bytes 1179656 | tf_op jit(solution)/shard_map/ppermute | solution.py:261
  29.4 18.3 %all-to-all-start = ((bf16[4,2,128,256]{3,2,1,0:T(8,128)(2,1)}), bf16[4,2,128,256]{3,2,1,0:T(8,128)(2,1)S(1)}, u32[]{:S(2)}, u32[]{:S(2)}) async-start(bf16[4,2,128,256]{3,2,1,0:T(8,128)(2,1)} %get-tuple-element.41), calls=%async_computation | async-start | bytes 1048576 | tf_op jit(solution)/shard_map/all_to_all | solution.py:222
  37.6 23.9 %collective-permute-start.5 = (bf16[2,2,128,256]{3,2,1,0:T(8,128)(2,1)}, bf16[2,2,128,256]{3,2,1,0:T(8,128)(2,1)S(1)}, u32[]{:S(2)}, u32[]{:S(2)}) collective-permute-start(bf16[2,2,128,256]{3,2,1,0:T(8,128)(2,1)} %get-tuple-element.43), channel_id=1, source_target_pairs={{0,4},{1,5},{2,6},{3,7},{4,8},{5,9},{6,10},{7,11},{8,12},{9,13},{1... | collective-permute-start | bytes 786440 | tf_op jit(solution)/shard_map/ppermute | solution.py:212
  40.9 20.6 %collective-permute-start.6 = (bf16[2,2,128,256]{3,2,1,0:T(8,128)(2,1)}, bf16[2,2,128,256]{3,2,1,0:T(8,128)(2,1)S(1)}, u32[]{:S(2)}, u32[]{:S(2)}) collective-permute-start(bf16[2,2,128,256]{3,2,1,0:T(8,128)(2,1)} %get-tuple-element.44), channel_id=1, source_target_pairs={{0,12},{1,13},{2,14},{3,15},{4,0},{5,1},{6,2},{7,3},{8,4},{9,5},{1... | collective-permute-start | bytes 786440 | tf_op jit(solution)/shard_map/ppermute | solution.py:212
  44.1 17.5 %collective-permute-start.7 = (bf16[2,2,128,256]{3,2,1,0:T(8,128)(2,1)}, bf16[2,2,128,256]{3,2,1,0:T(8,128)(2,1)S(1)}, u32[]{:S(2)}, u32[]{:S(2)}) collective-permute-start(bf16[2,2,128,256]{3,2,1,0:T(8,128)(2,1)} %get-tuple-element.45), channel_id=1, source_target_pairs={{0,8},{1,9},{2,10},{3,11},{4,12},{5,13},{6,14},{7,15},{8,0},{9,1},... | collective-permute-start | bytes 786440 | tf_op jit(solution)/shard_map/ppermute | solution.py:212
  47.8 27.5 %collective-permute-start.8 = (bf16[2,128,256]{2,1,0:T(8,128)(2,1)S(1)}, bf16[2,128,256]{2,1,0:T(8,128)(2,1)S(1)}, u32[]{:S(2)}, u32[]{:S(2)}) collective-permute-start(bf16[2,128,256]{2,1,0:T(8,128)(2,1)S(1)} %reduce_sum.21), channel_id=1, source_target_pairs={{0,2},{1,3},{2,0},{3,1},{4,6},{5,7},{6,4},{7,5},{8,10},{9,11},{10,... | collective-permute-start | bytes 393224 | tf_op jit(solution)/shard_map/ppermute | solution.py:26
  62.7 20.9 %collective-permute-start.9 = (bf16[2,128,256]{2,1,0:T(8,128)(2,1)S(1)}, bf16[2,128,256]{2,1,0:T(8,128)(2,1)S(1)}, u32[]{:S(2)}, u32[]{:S(2)}) collective-permute-start(bf16[2,128,256]{2,1,0:T(8,128)(2,1)S(1)} %get-tuple-element.47), channel_id=1, source_target_pairs={{0,3},{1,0},{2,1},{3,2},{4,7},{5,4},{6,5},{7,6},{8,11},{9,8},{10,9... | collective-permute-start | bytes 393224 | tf_op jit(solution)/shard_map/ppermute | solution.py:26
  66.0 17.5 %collective-permute-start.10 = (bf16[2,128,256]{2,1,0:T(8,128)(2,1)S(1)}, bf16[2,128,256]{2,1,0:T(8,128)(2,1)S(1)}, u32[]{:S(2)}, u32[]{:S(2)}) collective-permute-start(bf16[2,128,256]{2,1,0:T(8,128)(2,1)S(1)} %get-tuple-element.48), channel_id=1, source_target_pairs={{0,1},{1,2},{2,3},{3,0},{4,5},{5,6},{6,7},{7,4},{8,9},{9,10},{10,1... | collective-permute-start | bytes 393224 | tf_op jit(solution)/shard_map/ppermute | solution.py:26
  71.9 11.7 %all-to-all-start.1 = ((bf16[4,2,128,256]{3,2,1,0:T(8,128)(2,1)}), bf16[4,2,128,256]{3,2,1,0:T(8,128)(2,1)S(1)}, u32[]{:S(2)}, u32[]{:S(2)}) async-start(bf16[4,2,128,256]{3,2,1,0:T(8,128)(2,1)} %get-tuple-element.46), calls=%async_computation.1 | async-start | bytes 1048576 | tf_op jit(solution)/shard_map/all_to_all | solution.py:222

commit v5 on v4

--- a/solution.py
+++ b/solution.py
@@ -18,7 +18,8 @@
 ANY = pl.BlockSpec(memory_space=pl.ANY)
 VMEM = pl.BlockSpec(memory_space=pltpu.VMEM)
 FIRST_ROWS = (2,)
-OTHER_ROWS = (1, 3, 0)
+OTHER_ROWS = (1, 3)
+OWN_ROWS = (0,)
 
 
 def along_z(x, by):
@@ -51,7 +52,8 @@
 
 
 def res_kernel(
-    pair_ref, val_ref, cond_ref, bands_ref, out_ref, in_ref, bands, val, cond, pair, dens, sems
+    pair_ref, val_ref, cond_ref, bands_ref, out_ref, in_ref, own_ref, bands, val, cond, pair, dens,
+    sems,
 ):
     rows, groups = pair.shape
     own = rows // (N_X * N_Z)
@@ -71,10 +73,10 @@
     read.wait()
     gives = []
     later = []
-    for ref, steps in ((out_ref, FIRST_ROWS), (in_ref, OTHER_ROWS)):
+    for ref, steps in ((out_ref, FIRST_ROWS), (in_ref, OTHER_ROWS), (own_ref, OWN_ROWS)):
         for x in range(N_X):
             for k, m in enumerate(steps):
-                owner_x = x if ref is out_ref else (x + my_x) % N_X
+                owner_x = (x + my_x) % N_X if ref is in_ref else x
                 owner = owner_x * N_Z + (my_z + m) % N_Z
                 source = pl.ds(pl.multiple_of(owner * own, own), own)
                 target = ref.at[pl.ds((x * len(steps) + k) * own, own), :]
@@ -173,15 +175,12 @@
         give.wait()
 
 
-def in_kernel(
-    left_ref, band_ref, out_0, out_1, out_2, out_3, own_ref, left, band, out, sems, out_sems
-):
+def in_kernel(left_ref, band_ref, out_0, out_1, out_2, out_3, left, band, out, sems, out_sems):
     rows = table_copies((left_ref, band_ref), (left, band), sems, 0)
     for copy in rows:
         copy.start()
     for copy in rows:
         copy.wait()
-    my_x = lax.axis_index("pw") // N_Z
     count, steps, own, cols = out.shape
     each = count // N_X
     gives = []
@@ -192,19 +191,23 @@
                 out[by * each + n, step] = total[
                     n * own : (n + 1) * own, step * cols : (step + 1) * cols
                 ]
-        owner = own_ref.at[pl.ds((my_x + by) % N_X, 1)]
-        gives += [
-            pltpu.make_async_copy(
-                out.at[pl.ds(by * each, each - 1)], ref, out_sems.at[2 * by]
-            ),
-            pltpu.make_async_copy(
-                out.at[pl.ds(by * each + each - 1, 1)], owner, out_sems.at[2 * by + 1]
-            ),
-        ]
-        gives[-2].start()
+        gives.append(
+            pltpu.make_async_copy(out.at[pl.ds(by * each, each)], ref, out_sems.at[by])
+        )
         gives[-1].start()
     for give in gives:
         give.wait()
+
+
+def own_kernel(left_ref, band_ref, out_ref, left, band, out, sems):
+    rows = table_copies((left_ref, band_ref), (left, band), sems, 2)
+    for copy in rows:
+        copy.start()
+    for copy in rows:
+        copy.wait()
+    half = out.shape[0] // 2
+    halves = (out_ref.at[pl.ds(0, half)], out_ref.at[pl.ds(half, half)])
+    give_product(left, band, out, halves, sems)
 
 
 def along_x(x, by):
@@ -241,10 +244,10 @@
     block = pltpu.VMEM(band_pair.shape, BF16)
     index = pltpu.VMEM(band_bands.shape, jnp.int32)
     band_shape = jax.ShapeDtypeStruct((2 * cols, depth), BF16)
-    left_out, left_in = call(
+    left_out, left_in, left_own = call(
         res_kernel,
         "res_rows",
-        tuple(jax.ShapeDtypeStruct((n, depth), BF16) for n in (few, many)),
+        tuple(jax.ShapeDtypeStruct((n, depth), BF16) for n in (few, many, few)),
         [ANY] * 4,
         [
             pltpu.VMEM(res_bands.shape, jnp.int32),
@@ -255,8 +258,8 @@
         ],
         2 * 10**9,
     )(res_pair, val_form, cond_form, res_bands)
-    far, far_bands, near_bands, from_even, left_out, left_in, tables = lax.optimization_barrier(
-        (far, far_bands, near_bands, from_even, left_out, left_in, tables)
+    far, far_bands, near_bands, from_even, left_out, left_in, left_own, tables = lax.optimization_barrier(
+        (far, far_bands, near_bands, from_even, left_out, left_in, left_own, tables)
     )
     from_odd = lax.ppermute(far, "blk", [(i + 1, i) for i in range(0, blocks, 2)])
     out_term, bands = call(
@@ -277,18 +280,17 @@
         ],
         2 * 10**9,
     )(left_out, far, from_even, from_odd, far_bands, near_bands, *tables)
-    *in_terms, own_terms = call(
+    in_terms = call(
         in_kernel,
         "in_term",
-        (jax.ShapeDtypeStruct((len(OTHER_ROWS) - 1, 2, own, cols), BF16),) * N_X
-        + (jax.ShapeDtypeStruct((N_X, 2, own, cols), BF16),),
+        (jax.ShapeDtypeStruct((len(OTHER_ROWS), 2, own, cols), BF16),) * N_X,
         [ANY] * 2,
         [
             pltpu.VMEM((many, depth), BF16),
             band,
             pltpu.VMEM((many // own, 2, own, cols), BF16),
             pltpu.SemaphoreType.DMA((2,)),
-            pltpu.SemaphoreType.DMA((2 * N_X,)),
+            pltpu.SemaphoreType.DMA((N_X,)),
         ],
         2 * 10**9,
     )(left_in, bands)
@@ -304,7 +306,20 @@
     to_1, to_3 = summed(0).astype(BF16), summed(1).astype(BF16)
     from_1 = along_z(to_1, 1)
     from_3 = along_z(to_3, 3)
-    own_terms, _, _ = lax.optimization_barrier((own_terms, to_1, to_3))
+    left_own, _, _ = lax.optimization_barrier((left_own, to_1, to_3))
+    own_terms = call(
+        own_kernel,
+        "own_term",
+        jax.ShapeDtypeStruct((N_X, 2, own, cols), BF16),
+        [ANY] * 2,
+        [
+            pltpu.VMEM((few, depth), BF16),
+            band,
+            pltpu.VMEM((N_X, 2, own, cols), BF16),
+            pltpu.SemaphoreType.DMA((4,)),
+        ],
+        10**8,
+    )(left_own, bands)
     total = jnp.sum(shares_over_x(own_terms).astype(F32), axis=0)
     taken = pl.pallas_call(
         taken_kernel,

time: 85 us -> 87 us (1.024)
  the two profiles are of different devices: /device:TPU:1 before, /device:TPU:2 now
where the time goes in v5:
time: 87 us; the launch traced here: 86.5 us
  starting transfers between devices  56.2 us (65%)
  Pallas kernels  15.7 us (18%)
  waiting for transfers between devices  12.3 us (14%)
  other arithmetic  2 us (2%)
    ppermute x3, starting transfers between devices, along_z(): return lax.ppermute(x, 'pw', pairs)  24 us
    ppermute x3, starting transfers between devices, along_x(): return lax.ppermute(x, 'pw', pairs)  9.82 us
    all_to_all x2, starting transfers between devices, shares_over_x(): return lax.all_to_all(pieces, 'pw', 0, 0, axis_index_groups=X_GROUPS)  9.78 us
    pallas_call x1, Pallas kernels, local(): call(res_kernel, 'res_rows', tuple((jax.ShapeDtypeStruct((n, depth), BF16...  5.07 us
    all_to_all x2, waiting for transfers between devices, shares_over_x(): return lax.all_to_all(pieces, 'pw', 0, 0, axis_index_groups=X_GROUPS)  4.79 us
    pallas_call x1, Pallas kernels, local(): call(out_kernel, 'out_term', (jax.ShapeDtypeStruct((few // own, 2, own, c...  3.9 us
    ppermute x1, starting transfers between devices, local(): far = lax.ppermute(band_pair, 'blk', far_on)  3.83 us
    ppermute x1, starting transfers between devices, local(): far_bands = lax.ppermute(band_bands, 'blk', far_on)  3.83 us
  transfers between devices with their start and end apart: 13, of which 5 were waited for; matrix products, arithmetic and copies ran while one was open for 1% of the time, Pallas kernels for 14%

profile of v5, /device:TPU:2, one launch (start us, length us, event | category | flops | bytes accessed | tf_op | source)
XLA Modules:
  0.0 86.5 jit_solution(16892989191257170701)
XLA Ops:
  0.0 1.8 %collective-permute-start.3 = (bf16[256,768]{1,0:T(8,128)(2,1)}, bf16[256,768]{1,0:T(8,128)(2,1)S(1)}, u32[]{:S(2)}, u32[]{:S(2)}) collective-permute-start(bf16[256,768]{1,0:T(8,128)(2,1)} %param.9), channel_id=1, source_target_pairs={{0,16},{32,48},{64,80},{96,112},{128,144},{160,176},{192,208},{224... | collective-permute-start | bytes 1179656 | tf_op jit(solution)/shard_map/ppermute | solution.py:239
  1.8 3.8 %collective-permute-start = (bf16[256,768]{1,0:T(8,128)(2,1)}, bf16[256,768]{1,0:T(8,128)(2,1)S(1)}, u32[]{:S(2)}, u32[]{:S(2)}) collective-permute-start(bf16[256,768]{1,0:T(8,128)(2,1)} %param.9), channel_id=1, source_target_pairs={{0,32},{16,48},{32,64},{48,80},{64,96},{80,112},{96,128},{112,144}... | collective-permute-start | bytes 1179656 | tf_op jit(solution)/shard_map/ppermute | solution.py:236
  5.6 1.9 %collective-permute-start.2 = (s32[3,256]{1,0:T(4,128)}, s32[3,256]{1,0:T(4,128)S(1)}, u32[]{:S(2)}, u32[]{:S(2)}) collective-permute-start(s32[3,256]{1,0:T(4,128)} %param.15), channel_id=1, source_target_pairs={{0,16},{16,32},{32,48},{48,64},{64,80},{80,96},{96,112},{112,128},... | collective-permute-start | bytes 9224 | tf_op jit(solution)/shard_map/ppermute | solution.py:238
  7.5 3.8 %collective-permute-start.1 = (s32[3,256]{1,0:T(4,128)}, s32[3,256]{1,0:T(4,128)S(1)}, u32[]{:S(2)}, u32[]{:S(2)}) collective-permute-start(s32[3,256]{1,0:T(4,128)} %param.15), channel_id=1, source_target_pairs={{0,32},{16,48},{32,64},{48,80},{64,96},{80,112},{96,128},{112,144}... | collective-permute-start | bytes 9224 | tf_op jit(solution)/shard_map/ppermute | solution.py:237
  11.4 5.1 %res_rows.1 = (bf16[512,896]{1,0:T(8,128)(2,1)}, bf16[1024,896]{1,0:T(8,128)(2,1)}, bf16[512,896]{1,0:T(8,128)(2,1)}) custom-call(bf16[2048,768]{1,0:T(8,128)(2,1)} %pair_ref.1, bf16[400,128]{1,0:T(8,128)(2,1)} %val_ref.2, bf16[600,128]{1,0:T(8,128)(2,1)} %cond_ref.2, s32[3,2048]{1,0:T(4,128)} %bands_ref.1), custom_call_target="tpu_custom_call" | custom-call | flops 2000000000 | bytes 1000000 | tf_op jit(solution)/shard_map/res_rows/pallas_call | solution.py:247
  16.4 1.9 %collective-permute-done.2.near_bands_ref = s32[3,256]{1,0:T(4,128)S(1)} collective-permute-done((s32[3,256]{1,0:T(4,128)}, s32[3,256]{1,0:T(4,128)S(1)}, u32[]{:S(2)}, u32[]{:S(2)}) %collective-permute-start.2) | collective-permute-done | bytes 3104 | tf_op jit(solution)/shard_map/ppermute | solution.py:238
  18.3 1.4 %collective-permute-done.1.far_bands_ref = s32[3,256]{1,0:T(4,128)S(1)} collective-permute-done((s32[3,256]{1,0:T(4,128)}, s32[3,256]{1,0:T(4,128)S(1)}, u32[]{:S(2)}, u32[]{:S(2)}) %collective-permute-start.1) | collective-permute-done | bytes 3104 | tf_op jit(solution)/shard_map/ppermute | solution.py:237
  19.7 0.0 collective-permute-done.3.even_ref
  19.7 0.0 collective-permute-done.far_ref
  19.7 1.3 %collective-permute-start.4 = (bf16[256,768]{1,0:T(8,128)(2,1)S(1)}, bf16[256,768]{1,0:T(8,128)(2,1)}, u32[]{:S(2)}, u32[]{:S(2)}) collective-permute-start(bf16[256,768]{1,0:T(8,128)(2,1)S(1)} %collective-permute-done.far_ref), channel_id=1, source_target_pairs={{16,0},{48,32},{80,64},{112,96},{144,128},{176,160},{208,192},{240... | collective-permute-start | bytes 1179656 | tf_op jit(solution)/shard_map/ppermute | solution.py:264
  21.0 2.4 %collective-permute-done.4.from_odd_ref = bf16[256,768]{1,0:T(8,128)(2,1)} collective-permute-done((bf16[256,768]{1,0:T(8,128)(2,1)S(1)}, bf16[256,768]{1,0:T(8,128)(2,1)}, u32[]{:S(2)}, u32[]{:S(2)}) %collective-permute-start.4) | collective-permute-done | bytes 393248 | tf_op jit(solution)/shard_map/ppermute | solution.py:264
  23.5 3.9 %out_term.1 = (bf16[4,2,128,256]{3,2,1,0:T(8,128)(2,1)}, bf16[512,896]{1,0:T(8,128)(2,1)}) custom-call(bf16[512,896]{1,0:T(8,128)(2,1)} %get-tuple-element.32.left_ref, bf16[256,768]{1,0:T(8,128)(2,1)} %copy-done.1, bf16[256,768]{1,0:T(8,128)(2,1)} %copy-done, bf16[256,768]{1,0:T(8,128)(2,1)} %collective-permute-done.4.from_odd_ref, s32[3,256]{1,0:T(4,128)} %copy-done.3, ...), custom_call_target="tpu_custom_call" | custom-call | flops 2000000000 | bytes 1000000 | tf_op jit(solution)/shard_map/out_term/pallas_call | solution.py:265
  27.4 4.9 %all-to-all-start = ((bf16[4,2,128,256]{3,2,1,0:T(8,128)(2,1)}), bf16[4,2,128,256]{3,2,1,0:T(8,128)(2,1)S(1)}, u32[]{:S(2)}, u32[]{:S(2)}) async-start(bf16[4,2,128,256]{3,2,1,0:T(8,128)(2,1)} %get-tuple-element.43), calls=%async_computation | async-start | bytes 1048576 | tf_op jit(solution)/shard_map/all_to_all | solution.py:225
  32.3 3.8 %in_term.1 = (bf16[2,2,128,256]{3,2,1,0:T(8,128)(2,1)}, bf16[2,2,128,256]{3,2,1,0:T(8,128)(2,1)}, bf16[2,2,128,256]{3,2,1,0:T(8,128)(2,1)}, bf16[2,2,128,256]{3,2,1,0:T(8,128)(2,1)}) custom-call(bf16[1024,896]{1,0:T(8,128)(2,1)} %get-tuple-element.31.left_ref, bf16[512,896]{1,0:T(8,128)(2,1)} %get-tuple-element.41.band_ref), custom_call_target="tpu_custom_call" | custom-call | flops 2000000000 | bytes 1000000 | tf_op jit(solution)/shard_map/in_term/pallas_call | solution.py:283
  36.1 3.4 %collective-permute-start.5 = (bf16[2,2,128,256]{3,2,1,0:T(8,128)(2,1)}, bf16[2,2,128,256]{3,2,1,0:T(8,128)(2,1)S(1)}, u32[]{:S(2)}, u32[]{:S(2)}) collective-permute-start(bf16[2,2,128,256]{3,2,1,0:T(8,128)(2,1)} %get-tuple-element.45), channel_id=1, source_target_pairs={{0,4},{1,5},{2,6},{3,7},{4,8},{5,9},{6,10},{7,11},{8,12},{9,13},{1... | collective-permute-start | bytes 786440 | tf_op jit(solution)/shard_map/ppermute | solution.py:215
  39.4 2.5 %collective-permute-start.6 = (bf16[2,2,128,256]{3,2,1,0:T(8,128)(2,1)}, bf16[2,2,128,256]{3,2,1,0:T(8,128)(2,1)S(1)}, u32[]{:S(2)}, u32[]{:S(2)}) collective-permute-start(bf16[2,2,128,256]{3,2,1,0:T(8,128)(2,1)} %get-tuple-element.46), channel_id=1, source_target_pairs={{0,12},{1,13},{2,14},{3,15},{4,0},{5,1},{6,2},{7,3},{8,4},{9,5},{1... | collective-permute-start | bytes 786440 | tf_op jit(solution)/shard_map/ppermute | solution.py:215
  41.9 4.0 %collective-permute-start.7 = (bf16[2,2,128,256]{3,2,1,0:T(8,128)(2,1)}, bf16[2,2,128,256]{3,2,1,0:T(8,128)(2,1)S(1)}, u32[]{:S(2)}, u32[]{:S(2)}) collective-permute-start(bf16[2,2,128,256]{3,2,1,0:T(8,128)(2,1)} %get-tuple-element.47), channel_id=1, source_target_pairs={{0,8},{1,9},{2,10},{3,11},{4,12},{5,13},{6,14},{7,15},{8,0},{9,1},... | collective-permute-start | bytes 786440 | tf_op jit(solution)/shard_map/ppermute | solution.py:215
  45.9 0.0 all-to-all-done
  45.9 0.1 reduce_sum.21
  46.0 14.3 %collective-permute-start.8 = (bf16[2,128,256]{2,1,0:T(8,128)(2,1)S(1)}, bf16[2,128,256]{2,1,0:T(8,128)(2,1)S(1)}, u32[]{:S(2)}, u32[]{:S(2)}) collective-permute-start(bf16[2,128,256]{2,1,0:T(8,128)(2,1)S(1)} %reduce_sum.21), channel_id=1, source_target_pairs={{0,2},{1,3},{2,0},{3,1},{4,6},{5,7},{6,4},{7,5},{8,10},{9,11},{10,... | collective-permute-start | bytes 393224 | tf_op jit(solution)/shard_map/ppermute | solution.py:27
  60.3 0.0 collective-permute-done.6
  60.3 0.0 collective-permute-done.7
  60.3 1.1 %fusion.1 = (bf16[2,128,256]{2,1,0:T(8,128)(2,1)S(1)}, bf16[2,128,256]{2,1,0:T(8,128)(2,1)S(1)}) fusion(bf16[2,2,128,256]{3,2,1,0:T(8,128)(2,1)S(1)} %collective-permute-done.7, bf16[2,2,128,256]{3,2,1,0:T(8,128)(2,1)S(1)} %collective-permute-done.6, bf16[2,2,128,256]{3,2,1,0:T(8,128)(2,1)S(1)} %collective-permute-done.5, ...), kind=kLoop, calls=%fused_computation.4 | loop fusion | flops 1048576 | bytes 1310720 | tf_op jit(solution)/shard_map/add | solution.py:304
  61.4 6.2 %collective-permute-start.9 = (bf16[2,128,256]{2,1,0:T(8,128)(2,1)S(1)}, bf16[2,128,256]{2,1,0:T(8,128)(2,1)S(1)}, u32[]{:S(2)}, u32[]{:S(2)}) collective-permute-start(bf16[2,128,256]{2,1,0:T(8,128)(2,1)S(1)} %get-tuple-element.49), channel_id=1, source_target_pairs={{0,3},{1,0},{2,1},{3,2},{4,7},{5,4},{6,5},{7,6},{8,11},{9,8},{10,9... | collective-permute-start | bytes 393224 | tf_op jit(solution)/shard_map/ppermute | solution.py:27
  67.7 3.5 %collective-permute-start.10 = (bf16[2,128,256]{2,1,0:T(8,128)(2,1)S(1)}, bf16[2,128,256]{2,1,0:T(8,128)(2,1)S(1)}, u32[]{:S(2)}, u32[]{:S(2)}) collective-permute-start(bf16[2,128,256]{2,1,0:T(8,128)(2,1)S(1)} %get-tuple-element.50), channel_id=1, source_target_pairs={{0,1},{1,2},{2,3},{3,0},{4,5},{5,6},{6,7},{7,4},{8,9},{9,10},{10,1... | collective-permute-start | bytes 393224 | tf_op jit(solution)/shard_map/ppermute | solution.py:27
  71.2 2.9 %own_term.1 = bf16[4,2,128,256]{3,2,1,0:T(8,128)(2,1)} custom-call(bf16[512,896]{1,0:T(8,128)(2,1)} %get-tuple-element.48.left_ref, bf16[512,896]{1,0:T(8,128)(2,1)} %get-tuple-element.41.band_ref), custom_call_target="tpu_custom_call" | custom-call | flops 100000000 | bytes 1000000 | tf_op jit(solution)/shard_map/own_term/pallas_call | solution.py:310
  74.1 4.9 %all-to-all-start.1 = ((bf16[4,2,128,256]{3,2,1,0:T(8,128)(2,1)}), bf16[4,2,128,256]{3,2,1,0:T(8,128)(2,1)S(1)}, u32[]{:S(2)}, u32[]{:S(2)}) async-start(bf16[4,2,128,256]{3,2,1,0:T(8,128)(2,1)} %own_term.1), calls=%async_computation.1 | async-start | bytes 1048576 | tf_op jit(solution)/shard_map/all_to_all | solution.py:225
  79.0 1.8 %collective-permute-done.9.second_ref = bf16[2,128,256]{2,1,0:T(8,128)(2,1)S(1)} collective-permute-done((bf16[2,128,256]{2,1,0:T(8,128)(2,1)S(1)}, bf16[2,128,256]{2,1,0:T(8,128)(2,1)S(1)}, u32[]{:S(2)}, u32[]{:S(2)}) %collective-permute-start.9) | collective-permute-done | bytes 131104 | tf_op jit(solution)/shard_map/ppermute | solution.py:27
  80.8 0.0 collective-permute-done.10.third_ref
  80.9 4.8 %all-to-all-done.1 = bf16[4,2,128,256]{3,2,1,0:T(8,128)(2,1)S(1)} async-done(((bf16[4,2,128,256]{3,2,1,0:T(8,128)(2,1)}), bf16[4,2,128,256]{3,2,1,0:T(8,128)(2,1)S(1)}, u32[]{:S(2)}, u32[]{:S(2)}) %all-to-all-start.1) | async-done | bytes 524320 | tf_op jit(solution)/shard_map/all_to_all | solution.py:225
  85.6 0.1 convert_reduce_fusion
  85.7 0.7 add.39
  (11 shorter events, 0.1 us)
Async XLA Ops:
  0.0 19.7 %collective-permute-start.3 = (bf16[256,768]{1,0:T(8,128)(2,1)}, bf16[256,768]{1,0:T(8,128)(2,1)S(1)}, u32[]{:S(2)}, u32[]{:S(2)}) collective-permute-start(bf16[256,768]{1,0:T(8,128)(2,1)} %param.9), channel_id=1, source_target_pairs={{0,16},{32,48},{64,80},{96,112},{128,144},{160,176},{192,208},{224... | collective-permute-start | bytes 1179656 | tf_op jit(solution)/shard_map/ppermute | solution.py:239
  1.8 18.0 %collective-permute-start = (bf16[256,768]{1,0:T(8,128)(2,1)}, bf16[256,768]{1,0:T(8,128)(2,1)S(1)}, u32[]{:S(2)}, u32[]{:S(2)}) collective-permute-start(bf16[256,768]{1,0:T(8,128)(2,1)} %param.9), channel_id=1, source_target_pairs={{0,32},{16,48},{32,64},{48,80},{64,96},{80,112},{96,128},{112,144}... | collective-permute-start | bytes 1179656 | tf_op jit(solution)/shard_map/ppermute | solution.py:236
  5.6 12.7 %collective-permute-start.2 = (s32[3,256]{1,0:T(4,128)}, s32[3,256]{1,0:T(4,128)S(1)}, u32[]{:S(2)}, u32[]{:S(2)}) collective-permute-start(s32[3,256]{1,0:T(4,128)} %param.15), channel_id=1, source_target_pairs={{0,16},{16,32},{32,48},{48,64},{64,80},{80,96},{96,112},{112,128},... | collective-permute-start | bytes 9224 | tf_op jit(solution)/shard_map/ppermute | solution.py:238
  7.5 12.2 %collective-permute-start.1 = (s32[3,256]{1,0:T(4,128)}, s32[3,256]{1,0:T(4,128)S(1)}, u32[]{:S(2)}, u32[]{:S(2)}) collective-permute-start(s32[3,256]{1,0:T(4,128)} %param.15), channel_id=1, source_target_pairs={{0,32},{16,48},{32,64},{48,80},{64,96},{80,112},{96,128},{112,144}... | collective-permute-start | bytes 9224 | tf_op jit(solution)/shard_map/ppermute | solution.py:237
  18.3 5.2 %copy-start.2 = (s32[3,256]{1,0:T(4,128)}, s32[3,256]{1,0:T(4,128)S(1)}, u32[]{:S(2)}) copy-start(s32[3,256]{1,0:T(4,128)S(1)} %collective-permute-done.2.near_bands_ref) | copy-start | bytes 9220
  19.7 3.8 %copy-start.3 = (s32[3,256]{1,0:T(4,128)}, s32[3,256]{1,0:T(4,128)S(1)}, u32[]{:S(2)}) copy-start(s32[3,256]{1,0:T(4,128)S(1)} %collective-permute-done.1.far_bands_ref) | copy-start | bytes 9220
  19.7 3.8 %copy-start = (bf16[256,768]{1,0:T(8,128)(2,1)}, bf16[256,768]{1,0:T(8,128)(2,1)S(1)}, u32[]{:S(2)}) copy-start(bf16[256,768]{1,0:T(8,128)(2,1)S(1)} %collective-permute-done.3.even_ref) | copy-start | bytes 1179652
  19.7 3.8 %copy-start.1 = (bf16[256,768]{1,0:T(8,128)(2,1)}, bf16[256,768]{1,0:T(8,128)(2,1)S(1)}, u32[]{:S(2)}) copy-start(bf16[256,768]{1,0:T(8,128)(2,1)S(1)} %collective-permute-done.far_ref) | copy-start | bytes 1179652
  19.7 3.7 %collective-permute-start.4 = (bf16[256,768]{1,0:T(8,128)(2,1)S(1)}, bf16[256,768]{1,0:T(8,128)(2,1)}, u32[]{:S(2)}, u32[]{:S(2)}) collective-permute-start(bf16[256,768]{1,0:T(8,128)(2,1)S(1)} %collective-permute-done.far_ref), channel_id=1, source_target_pairs={{16,0},{48,32},{80,64},{112,96},{144,128},{176,160},{208,192},{240... | collective-permute-start | bytes 1179656 | tf_op jit(solution)/shard_map/ppermute | solution.py:264
  27.4 18.5 %all-to-all-start = ((bf16[4,2,128,256]{3,2,1,0:T(8,128)(2,1)}), bf16[4,2,128,256]{3,2,1,0:T(8,128)(2,1)S(1)}, u32[]{:S(2)}, u32[]{:S(2)}) async-start(bf16[4,2,128,256]{3,2,1,0:T(8,128)(2,1)} %get-tuple-element.43), calls=%async_computation | async-start | bytes 1048576 | tf_op jit(solution)/shard_map/all_to_all | solution.py:225
  36.1 24.2 %collective-permute-start.5 = (bf16[2,2,128,256]{3,2,1,0:T(8,128)(2,1)}, bf16[2,2,128,256]{3,2,1,0:T(8,128)(2,1)S(1)}, u32[]{:S(2)}, u32[]{:S(2)}) collective-permute-start(bf16[2,2,128,256]{3,2,1,0:T(8,128)(2,1)} %get-tuple-element.45), channel_id=1, source_target_pairs={{0,4},{1,5},{2,6},{3,7},{4,8},{5,9},{6,10},{7,11},{8,12},{9,13},{1... | collective-permute-start | bytes 786440 | tf_op jit(solution)/shard_map/ppermute | solution.py:215
  39.4 20.8 %collective-permute-start.6 = (bf16[2,2,128,256]{3,2,1,0:T(8,128)(2,1)}, bf16[2,2,128,256]{3,2,1,0:T(8,128)(2,1)S(1)}, u32[]{:S(2)}, u32[]{:S(2)}) collective-permute-start(bf16[2,2,128,256]{3,2,1,0:T(8,128)(2,1)} %get-tuple-element.46), channel_id=1, source_target_pairs={{0,12},{1,13},{2,14},{3,15},{4,0},{5,1},{6,2},{7,3},{8,4},{9,5},{1... | collective-permute-start | bytes 786440 | tf_op jit(solution)/shard_map/ppermute | solution.py:215
  41.9 18.4 %collective-permute-start.7 = (bf16[2,2,128,256]{3,2,1,0:T(8,128)(2,1)}, bf16[2,2,128,256]{3,2,1,0:T(8,128)(2,1)S(1)}, u32[]{:S(2)}, u32[]{:S(2)}) collective-permute-start(bf16[2,2,128,256]{3,2,1,0:T(8,128)(2,1)} %get-tuple-element.47), channel_id=1, source_target_pairs={{0,8},{1,9},{2,10},{3,11},{4,12},{5,13},{6,14},{7,15},{8,0},{9,1},... | collective-permute-start | bytes 786440 | tf_op jit(solution)/shard_map/ppermute | solution.py:215
  46.0 33.0 %collective-permute-start.8 = (bf16[2,128,256]{2,1,0:T(8,128)(2,1)S(1)}, bf16[2,128,256]{2,1,0:T(8,128)(2,1)S(1)}, u32[]{:S(2)}, u32[]{:S(2)}) collective-permute-start(bf16[2,128,256]{2,1,0:T(8,128)(2,1)S(1)} %reduce_sum.21), channel_id=1, source_target_pairs={{0,2},{1,3},{2,0},{3,1},{4,6},{5,7},{6,4},{7,5},{8,10},{9,11},{10,... | collective-permute-start | bytes 393224 | tf_op jit(solution)/shard_map/ppermute | solution.py:27
  61.4 19.4 %collective-permute-start.9 = (bf16[2,128,256]{2,1,0:T(8,128)(2,1)S(1)}, bf16[2,128,256]{2,1,0:T(8,128)(2,1)S(1)}, u32[]{:S(2)}, u32[]{:S(2)}) collective-permute-start(bf16[2,128,256]{2,1,0:T(8,128)(2,1)S(1)} %get-tuple-element.49), channel_id=1, source_target_pairs={{0,3},{1,0},{2,1},{3,2},{4,7},{5,4},{6,5},{7,6},{8,11},{9,8},{10,9... | collective-permute-start | bytes 393224 | tf_op jit(solution)/shard_map/ppermute | solution.py:27
  67.7 13.2 %collective-permute-start.10 = (bf16[2,128,256]{2,1,0:T(8,128)(2,1)S(1)}, bf16[2,128,256]{2,1,0:T(8,128)(2,1)S(1)}, u32[]{:S(2)}, u32[]{:S(2)}) collective-permute-start(bf16[2,128,256]{2,1,0:T(8,128)(2,1)S(1)} %get-tuple-element.50), channel_id=1, source_target_pairs={{0,1},{1,2},{2,3},{3,0},{4,5},{5,6},{6,7},{7,4},{8,9},{9,10},{10,1... | collective-permute-start | bytes 393224 | tf_op jit(solution)/shard_map/ppermute | solution.py:27
  74.1 11.5 %all-to-all-start.1 = ((bf16[4,2,128,256]{3,2,1,0:T(8,128)(2,1)}), bf16[4,2,128,256]{3,2,1,0:T(8,128)(2,1)S(1)}, u32[]{:S(2)}, u32[]{:S(2)}) async-start(bf16[4,2,128,256]{3,2,1,0:T(8,128)(2,1)} %own_term.1), calls=%async_computation.1 | async-start | bytes 1048576 | tf_op jit(solution)/shard_map/all_to_all | solution.py:225
